TPU v7x, 128 devices: a whole 4x4x4 slice. The times are simulated.
128 devices in a mesh: row: 32 (over y, x_lo, z), col: 4 (over x_hi, core).
Axes of the slice: x: 4 (x_hi: 2, x_lo: 2; x = x_hi * 2 + x_lo), y: 4, z: 4, core: 2. Of those that a mesh axis runs over, the one named last changes fastest.
Arguments:
- tokens: bfloat16 [16384, 2048], P('row', 'col'), may hold values from -6 to 6
- w_query: bfloat16 [2048, 2048], P('row', 'col'), may hold values from -0.125 to 0.125
- key_value_weight: bfloat16 [2048, 512], P('row', 'col'), may hold values from -0.125 to 0.125
- w_output: bfloat16 [2048, 2048], P('col', 'row'), may hold values from -0.5 to 0.5
- w_gate: bfloat16 [2048, 5632], P('row', 'col'), may hold values from -0.125 to 0.125
- w_up: bfloat16 [2048, 5632], P('row', 'col'), may hold values from -0.125 to 0.125
- w_down: bfloat16 [5632, 2048], P('col', 'row'), may hold values from -0.078125 to 0.078125
- gain_attention: bfloat16 [2048], P('row'), may hold values from 0.5 to 1.5
- gain_mlp: bfloat16 [2048], P('row'), may hold values from 0.5 to 1.5
- segment: int32 [16384], P('row'), may hold values from 0 to 8, as said below
- position: int32 [16384], P('row'), may hold values from 0 to 511, as said below
- cotangent: bfloat16 [16384, 2048], P('row', 'col'), may hold values from -6 to 6
Outputs:
- mixed: bfloat16 [16384, 2048], P('row', 'col')
- input_grad: float32 [16384, 2048], P('row', 'col')
- grad_query: float32 [2048, 2048], P('row', 'col')
- grad_keyval: float32 [2048, 512], P('row', 'col')
- grad_output: float32 [2048, 2048], P('col', 'row')
- grad_gate: float32 [2048, 5632], P('row', 'col')
- grad_up: float32 [2048, 5632], P('row', 'col')
- grad_down: float32 [5632, 2048], P('col', 'row')
- grad_gain_attention: float32 [2048], P('row')
- grad_gain_mlp: float32 [2048], P('row')
Inputs may be any that keep to these rules, and one draw needn't show every extreme that they name: `segment`: within each sequence of 512 tokens document numbers start at 0 and rise by one at each document's first token; every document holds 60 to min(800, 512) tokens, except the last of a sequence, which is cut at the sequence's end. `position`: A token's place counted from its document's first token.
All inputs are finite; a program needn't handle non-finite values.
Results may differ from a plain program's by a relative error of at most 0.029.
Values may be sent and summed in bfloat16 or wider, within the bound.
No kernel may reach another device: no remote copies, remote signals or barrier semaphores. Data moves between devices by JAX's collectives and lax.ppermute only.
A program may use at most 128 MiB of HBM per device.

v0:
```python
import math

import jax
import jax.numpy as jnp
from jax import lax
from jax.sharding import PartitionSpec as P

HEAD_SIZE = 64


EPSILON = 1e-05


def product(left, right):
    return jnp.dot(left, right, preferred_element_type=jnp.float32)


def rope_tables(position):
    half_width = HEAD_SIZE // 2
    steps_index = jnp.arange(half_width).astype(jnp.float32)
    frequency = jnp.exp(steps_index * (-2.0 * math.log(10000.0) / HEAD_SIZE))
    angles = position.astype(jnp.float32)[:, None, None] * frequency[None, None, :]
    return (jnp.cos(angles), jnp.sin(angles))


def rotate(values, cosine_table, sine_table):
    half_width = HEAD_SIZE // 2
    first = values[..., :half_width]
    second = values[..., half_width:]
    return jnp.concatenate(
        [first * cosine_table - second * sine_table, second * cosine_table + first * sine_table], -1
    )


def rotate_back(grads, cosine_table, sine_table):
    half_width = HEAD_SIZE // 2
    first = grads[..., :half_width]
    second = grads[..., half_width:]
    return jnp.concatenate(
        [first * cosine_table + second * sine_table, second * cosine_table - first * sine_table], -1
    )


def norm_back(upstream, unit, rms_value):
    return rms_value * (upstream - unit * jnp.mean(upstream * unit, -1, keepdims=True))


def shards(
    tokens,
    w_query,
    key_value_weight,
    w_output,
    w_gate,
    w_up,
    w_down,
    gain_attention,
    gain_mlp,
    segment,
    position,
    cotangent,
):
    row_count = tokens.shape[0]
    local_width = tokens.shape[1]
    heads_local = w_query.shape[1] // HEAD_SIZE
    keyval_local = key_value_weight.shape[1] // (2 * HEAD_SIZE)
    group_width = heads_local // keyval_local
    score_scale = 1.0 / math.sqrt(HEAD_SIZE)
    cosine_table, sine_table = rope_tables(position)
    token_place = jnp.arange(row_count)
    allowed = (segment[:, None] == segment[None, :]) & (
        token_place[:, None] >= token_place[None, :]
    )
    x_full = lax.all_gather(tokens, "col", axis=1, tiled=True)
    x_float = x_full.astype(jnp.float32)
    rms_one = lax.rsqrt(jnp.mean(x_float * x_float, -1, keepdims=True) + EPSILON)
    unit_one = x_float * rms_one
    pieces = (
        lax.all_gather(w_query, "row", axis=0, tiled=True),
        lax.all_gather(key_value_weight, "row", axis=0, tiled=True),
        lax.all_gather(gain_attention, "row", axis=0, tiled=True),
    )
    columns = unit_one
    normed = (columns * pieces[2].astype(jnp.float32)[None, :]).astype(jnp.bfloat16)
    query_proj = product(normed, pieces[0])
    key_value_projected = product(normed, pieces[1])
    rotated_query = rotate(
        query_proj.reshape(row_count, heads_local, HEAD_SIZE), cosine_table, sine_table
    ).astype(jnp.bfloat16)
    rotated_query = rotated_query.reshape(row_count, keyval_local, group_width, HEAD_SIZE)
    key_value_heads = key_value_projected.reshape(row_count, keyval_local, 2, HEAD_SIZE)
    rotated_key = rotate(key_value_heads[:, :, 0], cosine_table, sine_table).astype(jnp.bfloat16)
    value_reduced = key_value_heads[:, :, 1].astype(jnp.bfloat16)
    raw_scores = (
        jnp.einsum("qkgd,tkd->kgqt", rotated_query, rotated_key, preferred_element_type=jnp.float32)
        * score_scale
    )
    masked = jnp.where(allowed, raw_scores, -1e30)
    row_top = jnp.max(masked, -1, keepdims=True)
    exponent_terms = jnp.exp(masked - row_top)
    row_total = jnp.sum(exponent_terms, -1, keepdims=True)
    attn_probs = exponent_terms / row_total
    log_total = row_top + jnp.log(row_total)
    attended_rows = jnp.einsum(
        "kgqt,tkd->qkgd",
        attn_probs.astype(jnp.bfloat16),
        value_reduced,
        preferred_element_type=jnp.float32,
    )
    attended_rows = attended_rows.reshape(row_count, heads_local * HEAD_SIZE).astype(jnp.bfloat16)
    partial_attention = product(attended_rows, lax.all_gather(w_output, "row", axis=1, tiled=True))
    resid = tokens.astype(jnp.float32) + lax.psum_scatter(
        partial_attention, "col", scatter_dimension=1, tiled=True
    )
    resid_full = lax.all_gather(resid, "col", axis=1, tiled=True)
    rms_two = lax.rsqrt(jnp.mean(resid_full * resid_full, -1, keepdims=True) + EPSILON)
    unit_two = resid_full * rms_two
    pieces = (
        lax.all_gather(w_gate, "row", axis=0, tiled=True),
        lax.all_gather(w_up, "row", axis=0, tiled=True),
        lax.all_gather(gain_mlp, "row", axis=0, tiled=True),
    )
    columns = unit_two
    normed = (columns * pieces[2].astype(jnp.float32)[None, :]).astype(jnp.bfloat16)
    gate_value = product(normed, pieces[0])
    up_value = product(normed, pieces[1])
    sigmoid_gate = jax.nn.sigmoid(gate_value)
    activated = (gate_value * sigmoid_gate * up_value).astype(jnp.bfloat16)
    partial_mlp = product(activated, lax.all_gather(w_down, "row", axis=1, tiled=True))
    mixed = (
        resid
        + lax.psum_scatter(
            partial_mlp.astype(jnp.bfloat16), "col", scatter_dimension=1, tiled=True
        ).astype(jnp.float32)
    ).astype(jnp.bfloat16)
    full_weights = (
        lax.all_gather(w_query, "row", axis=0, tiled=True),
        lax.all_gather(key_value_weight, "row", axis=0, tiled=True),
        lax.all_gather(w_output, "row", axis=1, tiled=True),
        lax.all_gather(w_gate, "row", axis=0, tiled=True),
        lax.all_gather(w_up, "row", axis=0, tiled=True),
        lax.all_gather(w_down, "row", axis=1, tiled=True),
        lax.all_gather(gain_attention, "row", axis=0, tiled=True),
        lax.all_gather(gain_mlp, "row", axis=0, tiled=True),
    )
    (
        query_full,
        keyval_full,
        output_full,
        gate_full,
        up_full,
        down_full,
        gain_one_low,
        gain_two_low,
    ) = full_weights
    gain_one = gain_one_low.astype(jnp.float32)
    gain_two = gain_two_low.astype(jnp.float32)
    cot_full = lax.all_gather(cotangent, "col", axis=1, tiled=True)
    d_act = jnp.einsum("td,fd->tf", cot_full, down_full, preferred_element_type=jnp.float32)
    d_silu = d_act * up_value
    d_up = (d_act * (gate_value * sigmoid_gate)).astype(jnp.bfloat16)
    d_gate = (
        d_silu * sigmoid_gate + d_silu * gate_value * (sigmoid_gate * (1.0 - sigmoid_gate))
    ).astype(jnp.bfloat16)
    d_norm_two = lax.psum(
        jnp.einsum("tf,df->td", d_gate, gate_full, preferred_element_type=jnp.float32)
        + jnp.einsum("tf,df->td", d_up, up_full, preferred_element_type=jnp.float32),
        "col",
    )
    normed_two = (unit_two * gain_two).astype(jnp.bfloat16)
    grad_gate_rows = jnp.einsum("td,tf->df", normed_two, d_gate, preferred_element_type=jnp.float32)
    grad_up_rows = jnp.einsum("td,tf->df", normed_two, d_up, preferred_element_type=jnp.float32)
    grad_down_rows = jnp.einsum(
        "td,tf->df", cot_full, activated, preferred_element_type=jnp.float32
    )
    gain_two_term = jnp.sum(d_norm_two * unit_two, 0)
    mlp_grads = (
        lax.psum_scatter(
            grad_gate_rows.astype(jnp.bfloat16), "row", scatter_dimension=0, tiled=True
        ).astype(jnp.float32),
        lax.psum_scatter(
            grad_up_rows.astype(jnp.bfloat16), "row", scatter_dimension=0, tiled=True
        ).astype(jnp.float32),
        lax.psum_scatter(
            grad_down_rows.astype(jnp.bfloat16), "row", scatter_dimension=0, tiled=True
        ).astype(jnp.float32),
        lax.psum_scatter(
            gain_two_term.astype(jnp.bfloat16), "row", scatter_dimension=0, tiled=True
        ).astype(jnp.float32),
    )
    d_resid = cot_full.astype(jnp.float32) + norm_back(d_norm_two * gain_two, unit_two, rms_two)
    resid_low = d_resid.astype(jnp.bfloat16)
    d_attended = jnp.einsum(
        "td,jd->tj", resid_low, output_full, preferred_element_type=jnp.float32
    ).astype(jnp.bfloat16)
    d_attended = d_attended.reshape(row_count, keyval_local, group_width, HEAD_SIZE)
    grad_output_rows = jnp.einsum(
        "td,tj->dj", resid_low, attended_rows, preferred_element_type=jnp.float32
    )
    again_scores = (
        jnp.einsum("qkgd,tkd->kgqt", rotated_query, rotated_key, preferred_element_type=jnp.float32)
        * score_scale
    )
    again_probs = jnp.exp(jnp.where(allowed, again_scores, -1e30) - log_total)
    d_probs = jnp.einsum(
        "qkgd,tkd->kgqt", d_attended, value_reduced, preferred_element_type=jnp.float32
    )
    row_delta = jnp.sum(again_probs * d_probs, -1, keepdims=True)
    d_score = (again_probs * (d_probs - row_delta)).astype(jnp.bfloat16)
    d_query_rot = (
        jnp.einsum("kgqt,tkd->qkgd", d_score, rotated_key, preferred_element_type=jnp.float32)
        * score_scale
    )
    d_key_rot = (
        jnp.einsum("kgqt,qkgd->tkd", d_score, rotated_query, preferred_element_type=jnp.float32)
        * score_scale
    )
    d_value = jnp.einsum(
        "kgqt,qkgd->tkd",
        again_probs.astype(jnp.bfloat16),
        d_attended,
        preferred_element_type=jnp.float32,
    )
    d_query = rotate_back(
        d_query_rot.reshape(row_count, heads_local, HEAD_SIZE), cosine_table, sine_table
    )
    d_query = d_query.astype(jnp.bfloat16).reshape(row_count, heads_local * HEAD_SIZE)
    d_key = rotate_back(d_key_rot, cosine_table, sine_table)
    d_keyval = (
        jnp.stack([d_key, d_value], 2)
        .astype(jnp.bfloat16)
        .reshape(row_count, keyval_local * 2 * HEAD_SIZE)
    )
    d_norm_one = lax.psum(
        (
            jnp.einsum("tj,dj->td", d_query, query_full, preferred_element_type=jnp.float32)
            + jnp.einsum("tj,dj->td", d_keyval, keyval_full, preferred_element_type=jnp.float32)
        ).astype(jnp.bfloat16),
        "col",
    ).astype(jnp.float32)
    normed_one = (unit_one * gain_one).astype(jnp.bfloat16)
    grad_query_rows = jnp.einsum(
        "td,tj->dj", normed_one, d_query, preferred_element_type=jnp.float32
    )
    grad_keyval_rows = jnp.einsum(
        "td,tj->dj", normed_one, d_keyval, preferred_element_type=jnp.float32
    )
    gain_one_term = jnp.sum(d_norm_one * unit_one, 0)
    attention_grads = (
        lax.psum_scatter(
            grad_query_rows.astype(jnp.bfloat16), "row", scatter_dimension=0, tiled=True
        ).astype(jnp.float32),
        lax.psum_scatter(
            grad_keyval_rows.astype(jnp.bfloat16), "row", scatter_dimension=0, tiled=True
        ).astype(jnp.float32),
        lax.psum_scatter(
            grad_output_rows.astype(jnp.bfloat16), "row", scatter_dimension=0, tiled=True
        ).astype(jnp.float32),
        lax.psum_scatter(
            gain_one_term.astype(jnp.bfloat16), "row", scatter_dimension=0, tiled=True
        ).astype(jnp.float32),
    )
    d_input_full = d_resid + norm_back(d_norm_one * gain_one, unit_one, rms_one)
    input_grad = lax.dynamic_slice_in_dim(
        d_input_full, lax.axis_index("col") * local_width, local_width, 1
    )
    return (
        mixed,
        input_grad,
        attention_grads[0],
        attention_grads[1],
        attention_grads[2].T,
        mlp_grads[0],
        mlp_grads[1],
        mlp_grads[2].T,
        attention_grads[3],
        mlp_grads[3],
    )


def solution(mesh):
    placed = (
        P("row", "col"),
        P("row", "col"),
        P("row", "col"),
        P("col", "row"),
        P("row", "col"),
        P("row", "col"),
        P("col", "row"),
        P("row"),
        P("row"),
        P("row"),
        P("row"),
        P("row", "col"),
    )
    return jax.shard_map(
        shards,
        mesh=mesh,
        in_specs=placed,
        out_specs=(
            P("row", "col"),
            P("row", "col"),
            P("row", "col"),
            P("row", "col"),
            P("col", "row"),
            P("row", "col"),
            P("row", "col"),
            P("col", "row"),
            P("row"),
            P("row"),
        ),
        check_vma=False,
    )
```

profile of v0, /device:TPU:1, one launch (start us, length us, event | category | flops | bytes accessed | tf_op | source)
XLA Modules:
  0.0 2165.9 jit_solution(14836366037695211712)
XLA Ops:
  11.1 73.9 %all_gather.43 = bf16[2048,128]{1,0:T(8,128)(2,1)S(1)} all-gather(bf16[64,128]{1,0:T(8,128)(2,1)} %param.14), channel_id=1, replica_groups=mesh['row'=32,'col'=4] {'row'}, dimensions={0}, use_global_device_ids=true | all-gather | bytes 540672 | tf_op jit(solution)/shard_map/all_gather | solution.py:79
  89.0 65.5 %all-reduce.5 = (bf16[2048]{0:T(1024)(128)(2,1)S(1)}, bf16[2048]{0:T(1024)(128)(2,1)}) all-reduce(bf16[2048]{0:T(1024)(128)(2,1)S(1)} %dynamic-update-slice, bf16[2048]{0:T(1024)(128)(2,1)S(1)} %dynamic-update-slice.1), channel_id=1, replica_groups=mesh['row'=32,'col'=4] {'row'}, use_global_device_ids=true, to_apply=%add | all-reduce | flops 4096 | bytes 16384
  160.3 13.6 all-gather.11.cloned.1.call-done
  183.4 145.8 %all-gather.13.cloned.1.call-done = bf16[512,2048]{0,1:T(8,128)(2,1)} async-done(((bf16[512,64]{0,1:T(8,128)(2,1)}), bf16[512,2048]{0,1:T(8,128)(2,1)}) %all-gather.13.cloned.1.call-update) | async-done | bytes 2097168 | tf_op jit(solution)/shard_map/all_gather | solution.py:110
  334.3 72.0 %reduce-scatter.11.cloned.1.call-done = f32[512,512]{1,0:T(8,128)} async-done(((f32[512,2048]{1,0:T(8,128)}), f32[512,512]{1,0:T(8,128)}) %reduce-scatter.11.cloned.1.call-update) | async-done | bytes 1048592 | tf_op jit(solution)/shard_map/reduce_scatter | solution.py:111
  412.0 35.2 %all-gather.15.cloned.1.call-done = f32[512,2048]{1,0:T(8,128)} async-done(((f32[512,512]{1,0:T(8,128)}), f32[512,2048]{1,0:T(8,128)}) %all-gather.15.cloned.1.call-update) | async-done | bytes 4194320 | tf_op jit(solution)/shard_map/all_gather | solution.py:114
  452.3 139.2 %all-gather.19.cloned.1.call-done = bf16[2048,1408]{1,0:T(8,128)(2,1)} async-done(((bf16[64,1408]{1,0:T(8,128)(2,1)}), bf16[2048,1408]{1,0:T(8,128)(2,1)}) %all-gather.19.cloned.1.call-update) | async-done | bytes 5767184 | tf_op jit(solution)/shard_map/all_gather | solution.py:119
  591.5 8.3 fusion.69
  599.8 155.4 %all-gather.17.cloned.1.call-done = bf16[2048,1408]{1,0:T(8,128)(2,1)} async-done(((bf16[64,1408]{1,0:T(8,128)(2,1)}), bf16[2048,1408]{1,0:T(8,128)(2,1)}) %all-gather.17.cloned.1.call-update) | async-done | bytes 5767184 | tf_op jit(solution)/shard_map/all_gather | solution.py:118
  755.1 8.2 fusion.68
  763.4 38.7 %all-gather.23.cloned.1.call-done = bf16[512,2048]{1,0:T(8,128)(2,1)} async-done(((bf16[512,512]{1,0:T(8,128)(2,1)}), bf16[512,2048]{1,0:T(8,128)(2,1)}) %all-gather.23.cloned.1.call-update) | async-done | bytes 2097168 | tf_op jit(solution)/shard_map/all_gather | solution.py:157
  802.1 144.5 %all-gather.21.cloned.1.call-done = bf16[1408,2048]{0,1:T(8,128)(2,1)} async-done(((bf16[1408,64]{0,1:T(8,128)(2,1)}), bf16[1408,2048]{0,1:T(8,128)(2,1)}) %all-gather.21.cloned.1.call-update) | async-done | bytes 5767184 | tf_op jit(solution)/shard_map/all_gather | solution.py:128
  946.7 10.4 multiply_convert_fusion.2
  976.9 103.0 %all-reduce.9.cloned.1.call-done = f32[512,2048]{1,0:T(8,128)} async-done(((f32[512,2048]{1,0:T(8,128)}), f32[512,2048]{1,0:T(8,128)}) %all-reduce.9.cloned.1.call-update) | async-done | bytes 4194320 | tf_op jit(solution)/shard_map/psum | solution.py:164
  1123.6 8.3 copy.36
  1132.0 7.9 convolution_convert_fusion.1
  1151.4 104.8 %reduce-scatter.17.cloned.1.call-done = bf16[64,128]{1,0:T(8,128)(2,1)} async-done(((bf16[2048,128]{1,0:T(8,128)(2,1)}), bf16[64,128]{1,0:T(8,128)(2,1)}) %reduce-scatter.17.cloned.1.call-update) | async-done | bytes 16400 | tf_op jit(solution)/shard_map/reduce_scatter | solution.py:252
  1257.5 82.0 %all-reduce.11.cloned.1.call-done = bf16[512,2048]{1,0:T(8,128)(2,1)} async-done(((bf16[512,2048]{1,0:T(8,128)(2,1)}), bf16[512,2048]{1,0:T(8,128)(2,1)}) %all-reduce.11.cloned.1.call-update) | async-done | bytes 2097168 | tf_op jit(solution)/shard_map/psum | solution.py:233
  1345.6 71.5 %all-reduce.4 = (bf16[2048]{0:T(1024)(128)(2,1)S(1)}, bf16[2048]{0:T(1024)(128)(2,1)S(1)}) all-reduce(bf16[2048]{0:T(1024)(128)(2,1)S(1)} %get-tuple-element.32, bf16[2048]{0:T(1024)(128)(2,1)S(1)} %get-tuple-element.30), channel_id=10, replica_groups=mesh['row'=32,'col'=4] {'row'}, use_global_device_ids=true, to_apply=%region_18.19.clone | all-reduce | flops 4096 | bytes 16384
  1420.8 59.7 %reduce-scatter.15.cloned.1.call-done = bf16[64,512]{1,0:T(8,128)(2,1)} async-done(((bf16[2048,512]{1,0:T(8,128)(2,1)}), bf16[64,512]{1,0:T(8,128)(2,1)}) %reduce-scatter.15.cloned.1.call-update) | async-done | bytes 65552 | tf_op jit(solution)/shard_map/reduce_scatter | solution.py:249
  1482.0 160.3 %reduce-scatter.19.cloned.1.call-done = bf16[64,512]{1,0:T(8,128)(2,1)} async-done(((bf16[2048,512]{1,0:T(8,128)(2,1)}), bf16[64,512]{1,0:T(8,128)(2,1)}) %reduce-scatter.19.cloned.1.call-update) | async-done | bytes 65552 | tf_op jit(solution)/shard_map/reduce_scatter | solution.py:255
  1643.9 171.0 %reduce-scatter.25.cloned.1.call-done = bf16[64,1408]{1,0:T(8,128)(2,1)} async-done(((bf16[2048,1408]{1,0:T(8,128)(2,1)}), bf16[64,1408]{1,0:T(8,128)(2,1)}) %reduce-scatter.25.cloned.1.call-update) | async-done | bytes 180240
  1817.1 168.2 %reduce-scatter.23.cloned.1.call-done = bf16[64,1408]{1,0:T(8,128)(2,1)} async-done(((bf16[2048,1408]{1,0:T(8,128)(2,1)}), bf16[64,1408]{1,0:T(8,128)(2,1)}) %reduce-scatter.23.cloned.1.call-update) | async-done | bytes 180240 | tf_op jit(solution)/shard_map/reduce_scatter | solution.py:180
  1986.9 170.0 %reduce-scatter.21.cloned.1.call-done = bf16[64,1408]{1,0:T(8,128)(2,1)} async-done(((bf16[2048,1408]{1,0:T(8,128)(2,1)}), bf16[64,1408]{1,0:T(8,128)(2,1)}) %reduce-scatter.21.cloned.1.call-update) | async-done | bytes 180240 | tf_op jit(solution)/shard_map/reduce_scatter | solution.py:177
  (179 shorter events, 131.6 us)
Async XLA Ops:
  7.2 147.3 %all-gather.9.cloned.1.call-start = ((), (), s32[]{:S(2)}) async-start(), calls=%async_computation.8 | async-start | bytes 2621440 | tf_op jit(solution)/shard_map/all_gather | solution.py:73
  7.9 166.0 %all-gather.11.cloned.1.call-start = ((), (), s32[]{:S(2)}) async-start(), calls=%async_computation.9 | async-start | bytes 2162688 | tf_op jit(solution)/shard_map/all_gather | solution.py:78
  8.7 320.6 %all-gather.13.cloned.1.call-start = ((), (), s32[]{:S(2)}) async-start(), calls=%async_computation.10 | async-start | bytes 2162688 | tf_op jit(solution)/shard_map/all_gather | solution.py:110
  9.4 396.8 %reduce-scatter.11.cloned.1.call-start = ((), (), s32[]{:S(2)}) async-start(), calls=%async_computation.11 | async-start | bytes 5242880 | tf_op jit(solution)/shard_map/reduce_scatter | solution.py:111
  9.5 167.4 %copy-start.30 = (f32[32]{0:T(128)}, f32[32]{0:T(128)S(1)}, u32[]{:S(2)}) copy-start(f32[32]{0:T(128)S(1)} %multiply_exponential_fusion) | copy-start | bytes 388
  10.2 166.7 %copy-start.24 = (f32[512]{0:T(512)}, f32[512]{0:T(512)S(1)}, u32[]{:S(2)}) copy-start(f32[512]{0:T(512)S(1)} %convert_element_type.170) | copy-start | bytes 6148
  85.0 91.9 %copy-start.12 = (bf16[2048,128]{1,0:T(8,128)(2,1)}, bf16[2048,128]{1,0:T(8,128)(2,1)S(1)}, u32[]{:S(2)}) copy-start(bf16[2048,128]{1,0:T(8,128)(2,1)S(1)} %all_gather.43) | copy-start | bytes 1572868
  183.4 150.8 %copy-start.8 = (bf16[64,8,512]{2,0,1:T(8,128)(2,1)}, bf16[64,8,512]{2,0,1:T(8,128)(2,1)S(1)}, u32[]{:S(2)}) copy-start(bf16[64,8,512]{2,0,1:T(8,128)(2,1)S(1)} %fusion.20) | copy-start | bytes 1572868
  334.2 72.0 %copy-start.10 = (bf16[512,512]{1,0:T(8,128)(2,1)S(1)}, bf16[512,512]{1,0:T(8,128)(2,1)}, u32[]{:S(2)}) copy-start(bf16[512,512]{1,0:T(8,128)(2,1)} %param.12) | copy-start | bytes 1572868
  334.2 77.8 %copy-start.32 = (bf16[2048]{0:T(1024)(128)(2,1)S(1)}, bf16[2048]{0:T(1024)(128)(2,1)}, u32[]{:S(2)}) copy-start(bf16[2048]{0:T(1024)(128)(2,1)} %get-tuple-element.37) | copy-start | bytes 12292
  334.2 112.9 %all-gather.15.cloned.1.call-start = ((), (), s32[]{:S(2)}) async-start(), calls=%async_computation.12 | async-start | bytes 5242880 | tf_op jit(solution)/shard_map/all_gather | solution.py:114
  408.6 182.9 %all-gather.19.cloned.1.call-start = ((), (), s32[]{:S(2)}) async-start(), calls=%async_computation.14 | async-start | bytes 5947392 | tf_op jit(solution)/shard_map/all_gather | solution.py:119
  409.2 346.0 %all-gather.17.cloned.1.call-start = ((), (), s32[]{:S(2)}) async-start(), calls=%async_computation.13 | async-start | bytes 5947392 | tf_op jit(solution)/shard_map/all_gather | solution.py:118
  409.9 392.2 %all-gather.23.cloned.1.call-start = ((), (), s32[]{:S(2)}) async-start(), calls=%async_computation.17 | async-start | bytes 2621440 | tf_op jit(solution)/shard_map/all_gather | solution.py:157
  410.7 536.0 %all-gather.21.cloned.1.call-start = ((), (), s32[]{:S(2)}) async-start(), calls=%async_computation.15 | async-start | bytes 5947392 | tf_op jit(solution)/shard_map/all_gather | solution.py:128
  411.4 668.4 %all-reduce.9.cloned.1.call-start = ((), (), s32[]{:S(2)}) async-start(), calls=%async_computation.18 | async-start | bytes 8388608 | tf_op jit(solution)/shard_map/psum | solution.py:164
  968.2 180.7 %reduce-scatter.13.cloned.1.call-start = ((), (), s32[]{:S(2)}) async-start(), calls=%async_computation.16 | async-start | bytes 2621440 | tf_op jit(solution)/shard_map/reduce_scatter | solution.py:131
  976.8 279.4 %reduce-scatter.17.cloned.1.call-start = ((), (), s32[]{:S(2)}) async-start(), calls=%async_computation.21 | async-start | bytes 540672 | tf_op jit(solution)/shard_map/reduce_scatter | solution.py:252
  1102.4 237.2 %all-reduce.11.cloned.1.call-start = ((), (), s32[]{:S(2)}) async-start(), calls=%async_computation.19 | async-start | bytes 4194304 | tf_op jit(solution)/shard_map/psum | solution.py:233
  1108.0 372.6 %reduce-scatter.15.cloned.1.call-start = ((), (), s32[]{:S(2)}) async-start(), calls=%async_computation.20 | async-start | bytes 2162688 | tf_op jit(solution)/shard_map/reduce_scatter | solution.py:249
  1110.9 531.5 %reduce-scatter.19.cloned.1.call-start = ((), (), s32[]{:S(2)}) async-start(), calls=%async_computation.22 | async-start | bytes 2162688 | tf_op jit(solution)/shard_map/reduce_scatter | solution.py:255
  1115.8 699.1 %reduce-scatter.25.cloned.1.call-start = ((), (), s32[]{:S(2)}) async-start(), calls=%async_computation.25 | async-start | bytes 5947392
  1131.9 853.3 %reduce-scatter.23.cloned.1.call-start = ((), (), s32[]{:S(2)}) async-start(), calls=%async_computation.24 | async-start | bytes 5947392 | tf_op jit(solution)/shard_map/reduce_scatter | solution.py:180
  1140.0 1016.9 %reduce-scatter.21.cloned.1.call-start = ((), (), s32[]{:S(2)}) async-start(), calls=%async_computation.23 | async-start | bytes 5947392 | tf_op jit(solution)/shard_map/reduce_scatter | solution.py:177
  (32 other events, 166.7 us)
Sparse Core Ops, SparseCore 0:
  9.7 30.9 all-gather.8
  42.3 131.5 all-gather.10
  175.5 153.6 all-gather.12
  334.3 71.8 reduce-scatter.10
  408.7 38.3 all-gather.14
  448.7 142.7 all-gather.18
  593.2 161.8 all-gather.16
  756.9 45.1 all-gather.22
  803.9 142.7 all-gather.20
  968.4 111.4 all-reduce.8
  1082.5 37.3 reduce-scatter.12
  1122.2 133.9 reduce-scatter.16
  1258.7 80.8 all-reduce.10
  1341.9 138.6 reduce-scatter.14
  1482.8 159.5 reduce-scatter.18
  1644.7 170.0 reduce-scatter.24
  1817.2 167.9 reduce-scatter.22
  1987.6 169.2 reduce-scatter.20
where the time goes:
time: 2200 us; the launch traced here: 2170 us
  waiting for transfers between devices  1770 us (80%)
  blocking collectives  211 us (10%)
  matrix products  106 us (5%)
  other arithmetic  43.3 us (2%)
    unnamed x19, waiting for transfers between devices  176 us
    reduce_scatter x1, waiting for transfers between devices, shards(): lax.psum_scatter(grad_gate_rows.astype(jnp.bfloat16), 'row', scatter_dime...  170 us
    reduce_scatter x1, waiting for transfers between devices, shards(): lax.psum_scatter(grad_up_rows.astype(jnp.bfloat16), 'row', scatter_dimens...  168 us
    reduce_scatter x1, waiting for transfers between devices, shards(): lax.psum_scatter(grad_output_rows.astype(jnp.bfloat16), 'row', scatter_di...  160 us
    all_gather x1, waiting for transfers between devices, shards(): lax.all_gather(w_gate, 'row', axis=0, tiled=True)  155 us
    all_gather x1, waiting for transfers between devices, shards(): lax.all_gather(w_output, 'row', axis=1, tiled=True)  146 us
    all_gather x1, waiting for transfers between devices, shards(): lax.all_gather(w_down, 'row', axis=1, tiled=True)  145 us
    all_gather x1, waiting for transfers between devices, shards(): lax.all_gather(w_up, 'row', axis=0, tiled=True)  139 us
  transfers between devices with their start and end apart: 18, of which 16 were waited for; matrix products, arithmetic and copies ran while one was open for 6% of the time, Pallas kernels for 0%

commit v1 on v0

v1 whole, which is shorter than its diff:
```python
import functools
import math

import jax
import jax.numpy as jnp
from jax import lax
from jax.experimental import pallas as pl
from jax.experimental.pallas import tpu as pltpu
from jax.sharding import Mesh, PartitionSpec as P

F32, BF16 = jnp.float32, jnp.bfloat16
HEAD = 64
HALF = HEAD // 2
SCALE = 1.0 / math.sqrt(HEAD)
EPSILON = 1e-05
MASKED = -1e30
AXES = ("y", "xl", "z", "xh", "core")
SIZES = (4, 2, 4, 2, 2)
ROW, COL = ("y", "xl", "z"), ("xh", "core")

SEQ = 512
QUERIES = 256
TOGETHER = 4
MODEL = 2048
BLOCK = 512
QROWS = 512
QKV = QROWS + 128
GAINS_AT = QKV + 512
GAINS = 32
FFN = 704


def turn(second, mask):
    pairs = []
    for i in range(32):
        shift = 1 if (i % 2 == 0) != second else 3
        pairs.append((i, i ^ (mask << shift)))
    return lambda v: lax.ppermute(v, ("y", "z", "core"), pairs)


def cross(second):
    pairs = []
    for i in range(8):
        near = (i % 2 == 0) != second
        pairs.append((i, i ^ (4 if near else 6)))
    return lambda v: lax.ppermute(v, ("xl", "xh", "core"), pairs)


def swap_core(v):
    return lax.ppermute(v, "core", [(0, 1), (1, 0)])


def swap_xh(v):
    return lax.ppermute(v, "xh", [(0, 1), (1, 0)])


def swap_both(v):
    return lax.ppermute(v, ("xh", "core"), [(i, i ^ 3) for i in range(4)])


def swap_xl(v):
    return lax.ppermute(v, "xl", [(0, 1), (1, 0)])


def narrow(v):
    return v.astype(BF16)


def wide(v):
    return v.astype(F32)


def gather_two(v, after):
    held = bundle([v] + [turn(False, mask)(v) for mask in (1, 2, 3)], after)
    near, far = turn(True, 1), turn(True, 3)
    from_near, from_far = near(held), far(held)
    first, last = halves(from_near, from_far)
    return held, from_near, far(first), near(last), from_far


def reduce_start(terms, after):
    low, high, one, three, own = terms
    return (*add_halves(one, three, turn(True, 1)(low), turn(True, 3)(high), after), own)


def reduce_end(one, three, own, after):
    parts = sum_blocks(own, turn(True, 1)(one), turn(True, 3)(three), after)
    return [parts[0]] + [turn(False, mask)(parts[mask]) for mask in (1, 2, 3)]


def dot(a, b, contract):
    return lax.dot_general(a, b, ((contract[:1], contract[1:]), ((), ())), preferred_element_type=F32)


def nn(a, b):
    return dot(a, b, (1, 0))


def nt(a, b):
    return dot(a, b, (1, 1))


def tn(a, b):
    return dot(a, b, (0, 0))


def params(mib=14):
    return pltpu.CompilerParams(vmem_limit_bytes=mib * 1024 * 1024)


def cost(us):
    return pl.CostEstimate(flops=int(us * 1.15e9), bytes_accessed=0, transcendentals=0)


def spec(shape, index=None):
    zeros = (0,) * len(shape)
    return pl.BlockSpec(shape, index if index is not None else (lambda *_: zeros))


def whole(*arrays):
    return [spec(a.shape) for a in arrays]


def out(*shape, dtype=BF16):
    return jax.ShapeDtypeStruct(shape, dtype)


def lane_low(shape):
    return lax.broadcasted_iota(jnp.int32, shape, 1) < 64


def pair(a, b):
    low = lane_low(a.shape)
    return jnp.where(low, a, pltpu.roll(b, 64, 1)), jnp.where(low, pltpu.roll(a, 64, 1), b)


def tie_kernel(*refs):
    pass


def tie(arrays, *after):
    count = len(arrays)
    return pl.pallas_call(
        tie_kernel,
        in_specs=[ANYWHERE] * (count + len(after)),
        out_specs=(ANYWHERE,) * count,
        out_shape=tuple(jax.ShapeDtypeStruct(v.shape, v.dtype) for v in arrays),
        input_output_aliases={k: k for k in range(count)},
        compiler_params=params(),
        cost_estimate=cost(1),
    )(*arrays, *after)


def inner(src, dst):
    t = [wide(src[:, k * 128 : (k + 1) * 128]) for k in range(4)]
    z0, z1 = pair(t[0], t[2])
    z2, z3 = pair(t[1], t[3])
    for k, value in enumerate((z0, z1, z2, z3)):
        dst[:, k * 128 : (k + 1) * 128] = narrow(value)


def column(row):
    n = row.shape[1]
    here = lax.broadcasted_iota(jnp.int32, (n, n), 0) == lax.broadcasted_iota(jnp.int32, (n, n), 1)
    return jnp.sum(jnp.where(here, wide(row[...]), 0.0), 1, keepdims=True)


def prepare_kernel(tokens, cot, w_q, w_kv, w_o, gain_a, gain_m, x_o, cot_o, rows_o):
    rows_o[:, :QROWS] = w_q[...]
    rows_o[:, QROWS:QKV] = w_kv[...]
    rows_o[:, QKV:GAINS_AT] = w_o[...]
    lane = lax.broadcasted_iota(jnp.int32, (64, GAINS), 1)
    gains = jnp.where(lane == 0, column(gain_a), jnp.where(lane == 1, column(gain_m), 0.0))
    rows_o[:, GAINS_AT:] = narrow(gains)
    inner(tokens, x_o)
    inner(cot, cot_o)


def prepare(tokens, cot, w_q, w_kv, w_o, gain_a, gain_m):
    shapes = (out(*tokens.shape), out(*cot.shape), out(64, GAINS_AT + GAINS))
    args = (tokens, cot, w_q, w_kv, w_o, gain_a[None, :], gain_m[None, :])
    return pl.pallas_call(
        prepare_kernel,
        in_specs=whole(*args),
        out_specs=tuple(whole(*shapes)),
        out_shape=shapes,
        compiler_params=params(),
        cost_estimate=cost(3),
    )(*args)


def shard_attention_kernel(where, mine, other, *refs):
    upper = where[6] == 1
    a, b = wide(mine[...]), wide(other[...])
    rows = jnp.concatenate([jnp.where(upper, b, a), jnp.where(upper, a, b)], 0)
    refs[-1][...] = narrow(rows.T)


def shard_attention(where, mine, other, after):
    shape = out(mine.shape[1], 128)
    return pl.pallas_call(
        shard_attention_kernel,
        in_specs=[SCALARS] + whole(mine, other) + [ANYWHERE] * len(after),
        out_specs=spec(shape.shape),
        out_shape=shape,
        compiler_params=params(),
        cost_estimate=cost(2),
    )(where, mine, other, *after)


def prepare_mlp_kernel(where, w_g, w_u, w_d, keep_o, pack_o, held):
    for k, w in enumerate((w_g, w_u, w_d)):
        value = wide(w[...])
        both = jnp.concatenate([value[:, :FFN], value[:, FFN:]], 0)
        held[k * FFN : (k + 1) * FFN] = both.T
    keep_o[...] = narrow(held[...])
    pack_o[...] = narrow(packed(held[...], where[6] == 1))


def prepare_mlp(where, w_g, w_u, w_d):
    rows = 3 * FFN
    shapes = (out(rows, 128), out(rows // 2, 128))
    return pl.pallas_call(
        prepare_mlp_kernel,
        in_specs=[SCALARS] + whole(w_g, w_u, w_d),
        out_specs=tuple(whole(*shapes)),
        out_shape=shapes,
        scratch_shapes=[pltpu.VMEM((rows, 128), F32)],
        compiler_params=params(),
        cost_estimate=cost(4),
    )(where, w_g, w_u, w_d)


def sum_terms_kernel(a, b, c, d, total_o):
    total_o[...] = narrow(wide(a[...]) + wide(b[...]) + wide(c[...]) + wide(d[...]))


def sum_terms(terms):
    shape = out(*terms[0].shape)
    return pl.pallas_call(
        sum_terms_kernel,
        in_specs=whole(*terms),
        out_specs=spec(shape.shape),
        out_shape=shape,
        compiler_params=params(),
        cost_estimate=cost(2),
    )(*terms)


def add_split_kernel(a, b, *outs):
    for k, ref in enumerate(outs):
        ref[...] = narrow(wide(a[k]) + wide(b[k]))


def add_cores(keep, send):
    shapes = (out(*keep.shape[1:]),) * keep.shape[0]
    return pl.pallas_call(
        add_split_kernel,
        in_specs=whole(keep, send),
        out_specs=tuple(whole(*shapes)),
        out_shape=shapes,
        compiler_params=params(),
        cost_estimate=cost(2),
    )(keep, swap_core(send))


def to_natural(v):
    z = [v[:, k * 128 : (k + 1) * 128] for k in range(4)]
    t0, t2 = pair(z[0], z[1])
    t1, t3 = pair(z[2], z[3])
    return jnp.concatenate([t0, t1, t2, t3], 1)


def fetch(table, blocks, target, sems, start):
    rows = target.shape[0]
    copies = []
    for j in range(4):
        for i in range(4):
            src = block_of(blocks, j, i)
            lanes = pl.multiple_of(table[4 * j + i], 128)
            copy = pltpu.make_async_copy(
                src.at[pl.ds(start, rows)], target.at[:, pl.ds(lanes, 128)], sems.at[len(copies)]
            )
            copy.start()
            copies.append(copy)
    return copies


def block_of(blocks, j, i):
    own, one, low, high, three = blocks
    if j == 2:
        return low.at[i] if i < 2 else high.at[i - 2]
    return (own, one, None, three)[j].at[i]


def wait(copies):
    for copy in copies:
        copy.wait()


ANYWHERE = pl.BlockSpec(memory_space=pl.ANY)
SCALARS = pl.BlockSpec(memory_space=pltpu.SMEM)


def halves_kernel(a, b, a_o, b_o):
    a_o[...] = a[...]
    b_o[...] = b[...]


def halves(a, b):
    block = (2,) + a.shape[1:]
    first = spec(block, lambda i: (0, 0, 0))
    return pl.pallas_call(
        halves_kernel,
        grid=(1,),
        in_specs=[first, spec(block, lambda i: (1, 0, 0))],
        out_specs=(first, first),
        out_shape=(out(*block),) * 2,
        compiler_params=params(),
        cost_estimate=cost(2),
    )(a, b)


def add_halves_kernel(one, three, low, high, *refs):
    one_o, three_o = refs[-2:]
    three_o[...] = narrow(wide(three[...]) + wide(low[...]))
    one_o[...] = narrow(wide(one[...]) + wide(high[...]))


def add_halves(one, three, low, high, after):
    block = (1,) + one.shape[1:]
    first, last = spec(block, lambda i: (i, 0, 0)), spec(block, lambda i: (2 + i, 0, 0))
    return pl.pallas_call(
        add_halves_kernel,
        grid=(2,),
        in_specs=[last, first, first, first] + [ANYWHERE] * len(after),
        out_specs=(last, first),
        out_shape=(out(*one.shape),) * 2,
        input_output_aliases={0: 0, 1: 1},
        compiler_params=params(),
        cost_estimate=cost(2),
    )(one, three, low, high, *after)


def sum_blocks_kernel(a, b, c, *refs):
    for k, ref in enumerate(refs[-4:]):
        ref[...] = narrow(wide(a[k]) + wide(b[k]) + wide(c[k]))


def sum_blocks(a, b, c, after):
    shapes = (out(*a.shape[1:]),) * 4
    return pl.pallas_call(
        sum_blocks_kernel,
        in_specs=whole(a, b, c) + [ANYWHERE] * len(after),
        out_specs=tuple(whole(*shapes)),
        out_shape=shapes,
        compiler_params=params(),
        cost_estimate=cost(3),
    )(a, b, c, *after)


def packed(v, upper):
    half = v.shape[0] // 2
    top, bottom = v[:half], v[half:]
    low = lane_low(top.shape)
    return jnp.where(
        upper,
        jnp.where(low, top, pltpu.roll(bottom, 64, 1)),
        jnp.where(low, pltpu.roll(top, 64, 1), bottom),
    )


def unpacked(v, upper):
    turned = pltpu.roll(v, 64, 1)
    return [jnp.where(upper, v, turned), jnp.where(upper, turned, v)]


def own_lanes(shape, upper):
    return lane_low(shape) != upper


def sum_pack_kernel(where, *refs, count):
    sum_o, pack_o = refs[-2:]
    total = wide(refs[0][...])
    for ref in refs[1:count]:
        total += wide(ref[...])
    sum_o[...] = total
    pack_o[...] = narrow(packed(total, where[6] == 1))


def sum_pack(where, parts, after):
    rows = parts[0].shape[0]
    shapes = (out(rows, 128, dtype=F32), out(rows // 2, 128))
    return pl.pallas_call(
        functools.partial(sum_pack_kernel, count=len(parts)),
        in_specs=[SCALARS] + whole(*parts) + [ANYWHERE] * len(after),
        out_specs=tuple(whole(*shapes)),
        out_shape=shapes,
        compiler_params=params(),
        cost_estimate=cost(2),
    )(where, *parts, *after)


def merge_kernel(where, keep, other, *refs):
    upper = where[6] == 1
    half = other.shape[0]
    for k, part in enumerate(unpacked(wide(other[...]), upper)):
        rows = slice(k * half, (k + 1) * half)
        refs[-1][rows] = narrow(
            jnp.where(own_lanes(part.shape, upper), wide(keep[rows, :]), part)
        )


def merge(where, keep, other, after):
    return pl.pallas_call(
        merge_kernel,
        in_specs=[SCALARS] + whole(keep, other) + [ANYWHERE] * len(after),
        out_specs=spec(keep.shape),
        out_shape=out(*keep.shape),
        compiler_params=params(),
        cost_estimate=cost(2),
    )(where, keep, other, *after)


def row_dot(weight, grad):
    return jnp.sum(wide(weight) * grad, -1, keepdims=True)


def finish_mlp_kernel(where, total, other, w_gate, w_up, gate_o, up_o, down_o, sum_o, held):
    upper = where[6] == 1
    half = other.shape[0]
    for k, part in enumerate(unpacked(wide(other[...]), upper)):
        rows = slice(k * half, (k + 1) * half)
        held[rows] = jnp.where(own_lanes(part.shape, upper), total[rows, :], part)
    for k, ref in enumerate((gate_o, up_o, down_o)):
        turned = held[k * FFN : (k + 1) * FFN].T
        ref[:, :FFN] = turned[:64]
        ref[:, FFN:] = turned[64:]
    sum_o[...] = row_dot(w_gate[...], gate_o[...]) + row_dot(w_up[...], up_o[...])


def finish_mlp(where, total, other, w_gate, w_up):
    shapes = (out(64, 2 * FFN, dtype=F32),) * 3 + (out(64, 1, dtype=F32),)
    return pl.pallas_call(
        finish_mlp_kernel,
        in_specs=[SCALARS] + whole(total, other, w_gate, w_up),
        out_specs=tuple(whole(*shapes)),
        out_shape=shapes,
        scratch_shapes=[pltpu.VMEM(total.shape, F32)],
        compiler_params=params(),
        cost_estimate=cost(4),
    )(where, total, other, w_gate, w_up)


def finish_attention_kernel(where, total, other, w_q, w_kv, q_o, kv_o, out_o, sum_o, held):
    upper = where[6] == 1
    half = other.shape[0]
    for k, part in enumerate(unpacked(wide(other[...]), upper)):
        rows = slice(k * half, (k + 1) * half)
        held[:, rows] = (total[rows, :] + pltpu.roll(part, 64, 1)).T
    mine = held[pl.ds(pl.multiple_of(where[6] * 64, 64), 64), :]
    q_o[...] = mine[:, :QROWS]
    kv_o[...] = mine[:, QROWS:QKV]
    out_o[...] = mine[:, QKV:]
    sum_o[...] = row_dot(w_q[...], q_o[...]) + row_dot(w_kv[...], kv_o[...])


def finish_attention(where, total, other, w_q, w_kv):
    shapes = tuple(out(64, n, dtype=F32) for n in (QROWS, QKV - QROWS, QROWS, 1))
    return pl.pallas_call(
        finish_attention_kernel,
        in_specs=[SCALARS] + whole(total, other, w_q, w_kv),
        out_specs=tuple(whole(*shapes)),
        out_shape=shapes,
        scratch_shapes=[pltpu.VMEM((128, total.shape[0]), F32)],
        compiler_params=params(),
        cost_estimate=cost(3),
    )(where, total, other, w_q, w_kv)


def rotated(v, cos, sin):
    a, b = v[:HALF], v[HALF:]
    return jnp.concatenate([a * cos - b * sin, b * cos + a * sin], 0)


def rotated_back(v, cos, sin):
    a, b = v[:HALF], v[HALF:]
    return jnp.concatenate([a * cos + b * sin, b * cos - a * sin], 0)


def bundle_kernel(*refs):
    for k in range(4):
        refs[-1][k] = refs[k][...]


def bundle(parts, after):
    shape = out(4, *parts[0].shape)
    return pl.pallas_call(
        bundle_kernel,
        in_specs=whole(*parts) + [ANYWHERE] * len(after),
        out_specs=spec(shape.shape),
        out_shape=shape,
        compiler_params=params(),
        cost_estimate=cost(2),
    )(*parts, *after)


def attention_kernel(table, x0, x1, x2, x3, cos, sin, segment, *refs):
    blocks, refs = refs[:5], refs[-20:]
    n_o, p_o, r_o, q_o, k_o, v_o, gains_o, o_o, keep_o, send_o = refs[:10]
    w, w_out, n, probs, bias, w_sems, out_sems, gain_sems, n_sem, p_sems = refs[10:]
    copies = fetch(table, blocks, gains_o, gain_sems, GAINS_AT)
    w_copies = fetch(table, blocks, w, w_sems, 0)
    out_copies = fetch(table, blocks, w_out, out_sems, QKV)
    x = wide(jnp.concatenate([x0[...], x1[...], x2[...], x3[...]], 1))
    r = lax.rsqrt(jnp.mean(x * x, -1, keepdims=True) + EPSILON)
    r_o[...] = r
    wait(copies)
    n[...] = narrow(x * r * wide(gains_o[0:1, :]))
    saved = [pltpu.make_async_copy(n, n_o, n_sem)]
    saved[0].start()

    shape = (SEQ, SEQ)
    key = lax.broadcasted_iota(jnp.int32, shape, 0)
    query = lax.broadcasted_iota(jnp.int32, shape, 1)
    allowed = (column(segment) == wide(segment[...])) & (key <= query)
    bias[...] = jnp.where(allowed, 0.0, MASKED)

    wait(w_copies)
    qkv = nt(w[...], n[...])
    c, s = cos[...], sin[...]
    for h in range(QROWS // HEAD):
        head = rotated(qkv[h * HEAD : (h + 1) * HEAD], c, s)
        q_o[h * HEAD : (h + 1) * HEAD, :] = narrow(head) * SCALE
    k_o[...] = narrow(rotated(qkv[QROWS : QROWS + HEAD], c, s))
    v_o[...] = narrow(qkv[QROWS + HEAD :])

    for first in range(0, QROWS // HEAD, TOGETHER):
        for start in range(0, SEQ, QUERIES):
            stop = start + QUERIES
            queries = slice(start, stop)
            for h in range(first, first + TOGETHER):
                rows = slice(h * HEAD, (h + 1) * HEAD)
                s = tn(k_o[:, :stop], q_o[rows, queries]) + bias[:stop, queries]
                e = jnp.exp(s - jnp.max(s, 0, keepdims=True))
                probs[h, :stop, queries] = narrow(e * (1.0 / jnp.sum(e, 0, keepdims=True)))
            for h in range(first, first + TOGETHER):
                rows = slice(h * HEAD, (h + 1) * HEAD)
                o_o[rows, queries] = narrow(nn(v_o[:, :stop], probs[h, :stop, queries]))
        some = pl.ds(first, TOGETHER)
        saved.append(pltpu.make_async_copy(probs.at[some], p_o.at[some], p_sems.at[first]))
        saved[-1].start()

    wait(out_copies)
    value = tn(o_o[...], w_out[...])
    for k in range(4):
        (keep_o, send_o)[k % 2][k // 2] = narrow(value[:, k * BLOCK : (k + 1) * BLOCK])
    wait(saved)


def attention(table, x, cos, sin, segment, blocks):
    heads = QROWS // HEAD
    shapes = (
        out(SEQ, 1, dtype=F32),
        out(QROWS, SEQ),
        out(HEAD, SEQ),
        out(HEAD, SEQ),
        out(GAINS, MODEL),
        out(QROWS, SEQ),
        out(2, SEQ, BLOCK),
        out(2, SEQ, BLOCK),
    )
    return pl.pallas_call(
        attention_kernel,
        in_specs=[SCALARS]
        + whole(*x, cos, sin, segment)
        + [ANYWHERE] * 5,
        out_specs=(ANYWHERE, ANYWHERE, *whole(*shapes)),
        out_shape=(out(SEQ, MODEL), out(heads, SEQ, SEQ), *shapes),
        scratch_shapes=[
            pltpu.VMEM((QKV, MODEL), BF16),
            pltpu.VMEM((QROWS, MODEL), BF16),
            pltpu.VMEM((SEQ, MODEL), BF16),
            pltpu.VMEM((heads, SEQ, SEQ), BF16),
            pltpu.VMEM((SEQ, SEQ), F32),
            pltpu.SemaphoreType.DMA((16,)),
            pltpu.SemaphoreType.DMA((16,)),
            pltpu.SemaphoreType.DMA((16,)),
            pltpu.SemaphoreType.DMA,
            pltpu.SemaphoreType.DMA((heads,)),
        ],
        compiler_params=params(28),
        cost_estimate=cost(14),
    )(table, *x, cos, sin, segment, *blocks)


def mlp_kernel(table, where, *refs):
    h_in, cot_in, gains, blocks, refs = refs[:8], refs[8:16], refs[16], refs[17:22], refs[22:]
    r_o, n_o, cot_o, act_o, dgu_o, keep_o, send_o = refs[:7]
    w, wd, h, cot, n, act, dgu, chunk, sems, wd_sems, saves = refs[7:]
    copies = fetch(table, blocks, w, sems, 0)
    wd_copies = fetch(table, blocks, wd, wd_sems, 2 * FFN)
    saved = []

    def save(src, dst):
        copy = pltpu.make_async_copy(src, dst, saves.at[len(saved)])
        copy.start()
        saved.append(copy)

    for part in range(2):
        tokens = pl.ds(part * SEQ, SEQ)
        for k in range(4):
            lanes = slice(k * BLOCK, (k + 1) * BLOCK)
            if part == 0:
                lanes = pl.ds(pl.multiple_of(where[k], BLOCK), BLOCK)
            h[:, lanes] = h_in[4 * part + k][...]
            cot[part, :, lanes] = cot_in[4 * part + k][...]
        save(cot.at[part], cot_o.at[tokens])
        hidden = wide(h[...])
        r = lax.rsqrt(jnp.mean(hidden * hidden, -1, keepdims=True) + EPSILON)
        r_o[...] = r
        n[part] = narrow(hidden * r * wide(gains[1:2, :]))
        save(n.at[part], n_o.at[tokens])
        if part == 0:
            wait(copies)
        both = nt(w[...], n[part])
        if part == 0:
            wait(wd_copies)
        d_out = nt(wd[...], cot[part])
        gate, up = both[:FFN], both[FFN:]
        g = jax.nn.sigmoid(gate)
        silu = gate * g
        act[part] = narrow(silu * up)
        save(act.at[part], act_o.at[:, tokens])
        dgu[part, :FFN] = narrow(d_out * up * (g + silu * (1.0 - g)))
        dgu[part, FFN:] = narrow(d_out * silu)
        save(dgu.at[part], dgu_o.at[:, tokens])
        d_n = tn(dgu[part], w[...])
        for k in range(4):
            chunk[4 * part + k] = narrow(d_n[:, k * BLOCK : (k + 1) * BLOCK])
            block = 2 + k // 2 if part else where[4 + k % 2] ^ (k // 2)
            save(chunk.at[4 * part + k], (keep_o, send_o)[k % 2].at[block])
    wait(saved)


def mlp(table, where, h, cot, gains, blocks):
    shapes = (
        out(2 * SEQ, MODEL),
        out(2 * SEQ, MODEL),
        out(FFN, 2 * SEQ),
        out(2 * FFN, 2 * SEQ),
        out(4, SEQ, BLOCK),
        out(4, SEQ, BLOCK),
    )
    return pl.pallas_call(
        mlp_kernel,
        in_specs=[SCALARS] * 2 + whole(*h, *cot, gains) + [ANYWHERE] * 5,
        out_specs=(spec((SEQ, 1)),) + (ANYWHERE,) * 6,
        out_shape=(out(SEQ, 1, dtype=F32), *shapes),
        scratch_shapes=[
            pltpu.VMEM((2 * FFN, MODEL), BF16),
            pltpu.VMEM((FFN, MODEL), BF16),
            pltpu.VMEM((SEQ, MODEL), BF16),
            pltpu.VMEM((2, SEQ, MODEL), BF16),
            pltpu.VMEM((2, SEQ, MODEL), BF16),
            pltpu.VMEM((2, FFN, SEQ), BF16),
            pltpu.VMEM((2, 2 * FFN, SEQ), BF16),
            pltpu.VMEM((8, SEQ, BLOCK), BF16),
            pltpu.SemaphoreType.DMA((16,)),
            pltpu.SemaphoreType.DMA((16,)),
            pltpu.SemaphoreType.DMA((16,)),
        ],
        compiler_params=params(42),
        cost_estimate=cost(30),
    )(table, where, *h, *cot, gains, *blocks)


def down_kernel(table, where, act, *refs):
    blocks, (keep_o, send_o, w, sems) = refs[:5], refs[-4:]
    wait(fetch(table, blocks, w, sems, 2 * FFN))
    value = tn(act[...], w[...])
    for k in range(4):
        lanes = slice(k * BLOCK, (k + 1) * BLOCK)
        to = (keep_o, send_o)[k % 2]
        to[where[4 + k % 2] ^ (k // 2)] = narrow(value[:SEQ, lanes])
        to[2 + k // 2] = narrow(value[SEQ:, lanes])


def down(table, where, act, blocks, after):
    shapes = (out(4, SEQ, BLOCK),) * 2
    return pl.pallas_call(
        down_kernel,
        in_specs=[SCALARS] * 2 + whole(act) + [ANYWHERE] * (5 + len(after)),
        out_specs=tuple(whole(*shapes)),
        out_shape=shapes,
        scratch_shapes=[pltpu.VMEM((FFN, MODEL), BF16), pltpu.SemaphoreType.DMA((16,))],
        compiler_params=params(20),
        cost_estimate=cost(7),
    )(table, where, act, *blocks, *after)


def scatter(table, source, outs, sems, row):
    rows = source.shape[0]
    low, high, one, three, own = outs
    blocks = own, one, low, high, three
    copies = []
    for j in range(4):
        for i in range(4):
            lanes = pl.multiple_of(table[4 * j + i], 128)
            copy = pltpu.make_async_copy(
                source.at[:, pl.ds(lanes, 128)],
                block_of(blocks, j, i).at[pl.ds(row, rows)],
                sems.at[len(copies)],
            )
            copy.start()
            copies.append(copy)
    return copies


def terms_shapes(rows):
    return (out(2, rows, 128),) * 2 + (out(4, rows, 128),) * 3


def grads_mlp_kernel(table, dgu_in, act_in, n_in, cot_in, *refs):
    outs, (dgu, act, n, cot, made, made_down, load_sems, sems, down_sems) = refs[-14:-9], refs[-9:]
    loads = [
        pltpu.make_async_copy(src, dst, load_sems.at[k])
        for k, (src, dst) in enumerate(((dgu_in, dgu), (n_in, n), (act_in, act), (cot_in, cot)))
    ]
    for load in loads:
        load.start()
    wait(loads[:2])
    made[...] = narrow(nn(dgu[...], n[...]))
    copies = scatter(table, made, outs, sems, 0)
    wait(loads[2:])
    made_down[...] = narrow(nn(act[...], cot[...]))
    copies += scatter(table, made_down, outs, down_sems, 2 * FFN)
    wait(copies)


def grads_mlp(table, dgu, act, n, cot, after):
    shapes = terms_shapes(3 * FFN)
    return pl.pallas_call(
        grads_mlp_kernel,
        in_specs=[SCALARS] + [ANYWHERE] * (4 + len(after)),
        out_specs=(ANYWHERE,) * len(shapes),
        out_shape=shapes,
        scratch_shapes=[
            pltpu.VMEM(dgu.shape, BF16),
            pltpu.VMEM(act.shape, BF16),
            pltpu.VMEM(n.shape, BF16),
            pltpu.VMEM(cot.shape, BF16),
            pltpu.VMEM((2 * FFN, MODEL), BF16),
            pltpu.VMEM((FFN, MODEL), BF16),
            pltpu.SemaphoreType.DMA((4,)),
            pltpu.SemaphoreType.DMA((16,)),
            pltpu.SemaphoreType.DMA((16,)),
        ],
        compiler_params=params(34),
        cost_estimate=cost(15),
    )(table, dgu, act, n, cot, *after)


def attention_back_kernel(table, *refs):
    a_in, h_in, cot_in, (r, gains), refs = refs[:4], refs[4:8], refs[8:12], refs[12:14], refs[14:]
    (q, k, v, o, cos, sin), (n_in, p_in), blocks, refs = refs[:6], refs[6:8], refs[8:13], refs[13:]
    x_in, refs = refs[:4], refs[4:]
    (r_one, *_), refs = refs[:1], refs[-27:]
    (dh_o, keep_o, send_o), outs, refs = refs[:3], refs[3:8], refs[8:]
    w, w_qkv, e, n, p, do, dq, dkv, dk, dv, made_out, made = refs[:12]
    w_sems, qkv_sems, out_sems, sems, load_sems, save_sems, chunk = refs[12:]
    qkv_copies = fetch(table, blocks, w_qkv, qkv_sems, 0)
    copies = fetch(table, blocks, w, w_sems, QKV)
    loads = [
        pltpu.make_async_copy(p_in, p, load_sems.at[0]),
        pltpu.make_async_copy(n_in, n, load_sems.at[1]),
    ]
    for load in loads:
        load.start()

    def joined(parts):
        return wide(jnp.concatenate([part[...] for part in parts], 1))

    scale = r[...]
    unit = joined(h_in) * scale
    a = joined(a_in) * wide(gains[1:2, :])
    d_h = joined(cot_in) + scale * (a - unit * jnp.mean(a * unit, -1, keepdims=True))
    dh_o[...] = d_h[:, :BLOCK]
    e[...] = narrow(d_h)
    wait(copies)
    do[...] = narrow(nt(w[...], e[...]))
    made_out[...] = narrow(nn(o[...], e[...]))
    scattered = scatter(table, made_out, outs, out_sems, QKV)

    loads[0].wait()
    dk[...] = jnp.zeros_like(dk)
    dv[...] = jnp.zeros_like(dv)
    for first in range(0, QROWS // HEAD, TOGETHER):
        for start in range(0, SEQ, QUERIES):
            stop = start + QUERIES
            queries = slice(start, stop)
            scores = []
            for h in range(first, first + TOGETHER):
                rows = slice(h * HEAD, (h + 1) * HEAD)
                probs = wide(p[h, :stop, queries])
                dp = tn(v[:, :stop], do[rows, queries])
                scores.append(narrow(probs * (dp - jnp.sum(probs * dp, 0, keepdims=True))))
            for h, ds in zip(range(first, first + TOGETHER), scores, strict=True):
                rows = slice(h * HEAD, (h + 1) * HEAD)
                d_q = nn(k[:, :stop], ds) * SCALE
                dq[rows, queries] = narrow(rotated_back(d_q, cos[:, queries], sin[:, queries]))
                dk[:, :stop] += nt(q[rows, queries], ds)
                dv[:, :stop] += nt(do[rows, queries], p[h, :stop, queries])
    dkv[:HEAD, :] = narrow(rotated_back(dk[...], cos[...], sin[...]))
    dkv[HEAD:, :] = narrow(dv[...])

    loads[1].wait()
    d = jnp.concatenate([dq[...], dkv[...]], 0)
    made[...] = narrow(nn(d, n[...]))
    scattered += scatter(table, made, outs, sems, 0)

    wait(qkv_copies)
    part = tn(d, w_qkv[...])
    product = narrow(part * (joined(x_in) * r_one[...] * wide(gains[0:1, :])))
    stat = narrow(nt(jnp.ones((16, MODEL), BF16), product))
    saved = []
    for k in range(4):
        chunk[k, :SEQ] = narrow(part[:, k * BLOCK : (k + 1) * BLOCK])
        chunk[k, SEQ:] = stat
        to = (keep_o, send_o)[k % 2].at[k // 2]
        saved.append(pltpu.make_async_copy(chunk.at[k], to, save_sems.at[k]))
        saved[-1].start()
    wait(saved)
    wait(scattered)


def attention_back(table, a, h, cot, r, gains, q, k, v, o, cos, sin, n, p, blocks, x, r_one, after):
    heads = QROWS // HEAD
    shapes = (out(SEQ, BLOCK, dtype=F32),)
    chunks = (out(2, SEQ + 16, BLOCK),) * 2
    return pl.pallas_call(
        attention_back_kernel,
        in_specs=[SCALARS]
        + whole(*a, *h, *cot, r, gains, q, k, v, o, cos, sin)
        + [ANYWHERE] * 7
        + whole(*x, r_one)
        + [ANYWHERE] * len(after),
        out_specs=(*whole(*shapes), *[ANYWHERE] * 7),
        out_shape=(*shapes, *chunks, *terms_shapes(GAINS_AT)),
        scratch_shapes=[
            pltpu.VMEM((QROWS, MODEL), BF16),
            pltpu.VMEM((QKV, MODEL), BF16),
            pltpu.VMEM((SEQ, MODEL), BF16),
            pltpu.VMEM((SEQ, MODEL), BF16),
            pltpu.VMEM((heads, SEQ, SEQ), BF16),
            pltpu.VMEM((QROWS, SEQ), BF16),
            pltpu.VMEM((QROWS, SEQ), BF16),
            pltpu.VMEM((2 * HEAD, SEQ), BF16),
            pltpu.VMEM((HEAD, SEQ), F32),
            pltpu.VMEM((HEAD, SEQ), F32),
            pltpu.VMEM((QROWS, MODEL), BF16),
            pltpu.VMEM((QKV, MODEL), BF16),
            pltpu.SemaphoreType.DMA((16,)),
            pltpu.SemaphoreType.DMA((16,)),
            pltpu.SemaphoreType.DMA((16,)),
            pltpu.SemaphoreType.DMA((16,)),
            pltpu.SemaphoreType.DMA((2,)),
            pltpu.SemaphoreType.DMA((4,)),
            pltpu.VMEM((4, SEQ + 16, BLOCK), BF16),
        ],
        compiler_params=params(34),
        cost_estimate=cost(22),
    )(table, *a, *h, *cot, r, gains, q, k, v, o, cos, sin, n, p, *blocks, *x, r_one, *after)


def outputs_kernel(h, m0, m1, m2, m3, dh, c0, c1, x, r, gains, *refs):
    mixed_o, grad_o = refs[-2:]
    m = wide(m0[...]) + wide(m1[...]) + wide(m2[...]) + wide(m3[...])
    mixed_o[...] = narrow(to_natural(h[...] + m))
    total = wide(c0[...]) + wide(c1[...])
    stat = total[SEQ:].T[:, :1] * (1.0 / MODEL)
    scale = r[...]
    c_full = total[:SEQ] * wide(gains[0:1, :])
    grad_o[...] = to_natural(dh[...] + scale * (c_full - wide(x[...]) * scale * stat))


def outputs(h, m, dh, c, x, r, gains, after):
    shapes = (out(SEQ, BLOCK), out(SEQ, BLOCK, dtype=F32))
    args = (h, *m, dh, *c, x, r)
    return pl.pallas_call(
        outputs_kernel,
        grid=(1,),
        in_specs=whole(*args) + [spec((GAINS, BLOCK))] + [ANYWHERE] * len(after),
        out_specs=tuple(whole(*shapes)),
        out_shape=shapes,
        compiler_params=params(),
        cost_estimate=cost(5),
    )(*args, gains, *after)


def spread_eight(own, opposite, first, second):
    return own, cross(False)(first), cross(True)(second), swap_xh(opposite)


def gather_four(v):
    other = swap_xh(v)
    return v, swap_core(v), other, swap_core(other)


def gather_other(v):
    first, second = cross(False), cross(True)
    a, b = first(v), second(v)
    return (a, swap_core(a), b, swap_core(b)), second(a)


def gather_own(v, opposite):
    return v, swap_core(v), opposite, swap_core(opposite)


def shards(
    tokens,
    w_query,
    key_value_weight,
    w_output,
    w_gate,
    w_up,
    w_down,
    gain_attention,
    gain_mlp,
    segment,
    position,
    cotangent,
):
    core = lax.axis_index("core")
    col = lax.axis_index("xh") * 2 + core
    upper = lax.axis_index("xl") == 1
    far, close = jnp.arange(4)[:, None], jnp.arange(4)[None, :]
    y = (lax.axis_index("y") ^ col) ^ jnp.where(core == 0, far, close)
    z = lax.axis_index("z") ^ jnp.where(core == 0, close, far)
    table = ((y * 4 + z) * 128).reshape(16).astype(jnp.int32)
    other_at = jnp.stack(
        [
            2 * BLOCK * core,
            BLOCK + 2 * BLOCK * (1 - core),
            2 * BLOCK * (1 - core),
            BLOCK + 2 * BLOCK * core,
            core,
            1 - core,
            lax.axis_index("xl"),
        ]
    ).astype(jnp.int32)

    x_own, cot_own, attn_rows = prepare(
        tokens, cotangent, w_query, key_value_weight, w_output.T, gain_attention, gain_mlp
    )
    mlp_keep, mlp_pack = prepare_mlp(other_at, w_gate, w_up, w_down.T)
    attn_shard = shard_attention(other_at, attn_rows, swap_xl(attn_rows), (mlp_pack,))
    x_all = gather_four(x_own)
    attn_blocks = gather_two(attn_shard, (mlp_pack,))
    mlp_shard = merge(
        other_at, mlp_keep, swap_xl(mlp_pack), (attn_blocks[1], attn_blocks[4])
    )
    cot_other, opposite = gather_other(cot_own)
    cot_self = gather_own(cot_own, opposite)

    frequency = jnp.exp(jnp.arange(HALF).astype(F32) * (-2.0 * math.log(10000.0) / HEAD))
    angles = frequency[:, None] * position.astype(F32)[None, :]
    cos, sin = jnp.cos(angles), jnp.sin(angles)
    normed_one, probs, r_one, q, k, v, gains, o, keep, send = attention(
        table, x_all, cos, sin, segment[None, :], attn_blocks
    )
    here, there = add_cores(keep, send)
    resid = wide(x_own) + wide(here) + wide(swap_xh(there))
    resid_low = narrow(resid)
    mlp_blocks = gather_two(mlp_shard, (r_one,))
    h_other, opposite = gather_other(resid_low)
    h_self = gather_own(resid_low, opposite)
    r_two, n, cot, act, dgu, keep, send = mlp(
        table, other_at, (*h_other, *h_self), (*cot_other, *cot_self), gains, mlp_blocks
    )
    sums = add_cores(keep, send)
    mlp_terms = grads_mlp(table, dgu, act, n, cot, sums[:1])
    d_normed_two = sum_terms(spread_eight(sums[2], sums[3], sums[0], sums[1]))
    mlp_terms = tie(mlp_terms, d_normed_two)
    keep, send = down(table, other_at, act, mlp_blocks, (d_normed_two,))
    (opposite,) = tie((swap_xh(d_normed_two),), keep)
    keep, send = tie((keep, send), opposite)
    d_normed_all = gather_own(d_normed_two, opposite)
    mlp_terms = reduce_start(mlp_terms, ())
    sum_out = add_cores(keep, send)
    mlp_out = spread_eight(sum_out[2], sum_out[3], sum_out[0], sum_out[1])
    d_resid, keep, send, *attn_terms = attention_back(
        table,
        d_normed_all,
        h_self,
        cot_self,
        r_two,
        gains,
        q,
        k,
        v,
        o,
        cos,
        sin,
        normed_one,
        probs,
        attn_blocks,
        x_all,
        r_one,
        mlp_terms[:1],
    )
    here, there = add_cores(keep, send)

    d_normed_one = here, swap_xh(there)
    mlp_parts = reduce_end(*mlp_terms, ())
    attn_terms = reduce_start(attn_terms, (here, mlp_parts[0]))
    attn_parts = reduce_end(*attn_terms, d_normed_one[1:])
    mlp_total, mlp_pack = sum_pack(other_at, mlp_parts, attn_terms[:1])
    mixed, input_grad = outputs(
        resid, mlp_out, d_resid, d_normed_one, x_own, r_one, gains, attn_parts[:1]
    )
    attn_total, attn_pack = sum_pack(other_at, attn_parts, (mixed,))
    grad_gate, grad_up, grad_down, sum_two = finish_mlp(
        other_at, mlp_total, swap_xl(mlp_pack), w_gate, w_up
    )
    grad_query, grad_keyval, grad_output, sum_one = finish_attention(
        other_at, attn_total, swap_xl(attn_pack), w_query, key_value_weight
    )
    sums = jnp.concatenate([sum_one, sum_two], 0).reshape(1, 128)
    sums = (sums + swap_core(sums) + swap_xh(sums) + swap_both(sums)).reshape(2, 64)
    gain_one = sums[0] / wide(gain_attention)
    gain_two = sums[1] / wide(gain_mlp)
    return (
        mixed,
        input_grad,
        grad_query,
        grad_keyval,
        grad_output.T,
        grad_gate,
        grad_up,
        grad_down.T,
        gain_one,
        gain_two,
    )


def solution(mesh):
    fine = Mesh(mesh.devices.reshape(SIZES), AXES)
    both, turned, rows = P(ROW, COL), P(COL, ROW), P(ROW)
    return jax.shard_map(
        shards,
        mesh=fine,
        in_specs=(both, both, both, turned, both, both, turned, rows, rows, rows, rows, both),
        out_specs=(both, both, both, both, turned, both, both, turned, rows, rows),
        check_vma=False,
    )
```

time: 2200 us -> 347 us (0.16); the launches traced: 2170 us -> 341 us
  waiting for transfers between devices: 1770 us -> 104 us
  blocking collectives: 211 us -> 0 us
  starting transfers between devices: 1.82 us -> 112 us
  matrix products: 106 us -> 0 us
  Pallas kernels: 0 us -> 92.3 us
  other arithmetic: 43.3 us -> 1.23 us
    reduce_scatter x7 -> x0, waiting for transfers between devices: 735 us -> none  [the longest x1 170 us: shards(): lax.psum_scatter(grad_gate_rows.astype(jnp.bfloat16), 'row', scatter_dime...]
    all_gather x8 -> x0, waiting for transfers between devices: 672 us -> none  [the longest x1 155 us: shards(): lax.all_gather(w_gate, 'row', axis=0, tiled=True)]
    psum x2 -> x0, waiting for transfers between devices: 185 us -> none  [the longest x1 103 us: shards(): lax.psum(jnp.einsum('tf,df->td', d_gate, gate_full, preferred_element_typ...]
    unnamed x19 -> x0, waiting for transfers between devices: 176 us -> none
    unnamed x2 -> x0, blocking collectives: 137 us -> none
    ppermute x0 -> x67, starting transfers between devices: none -> 112 us  [the longest x17 50 us: swap_core(): return lax.ppermute(v, 'core', [(0, 1), (1, 0)])]
    dot_general x24 -> x0, matrix products: 106 us -> none  [the longest x6 34.7 us: product(): return jnp.dot(left, right, preferred_element_type=jnp.float32)]
    ppermute x0 -> x67, waiting for transfers between devices: none -> 104 us  [the longest x28 41.5 us: turn(): return lambda v: lax.ppermute(v, ('y', 'z', 'core'), pairs)]
  transfers between devices with their start and end apart: 18 -> 67, of which waited for: 16 -> 30; matrix products, arithmetic and copies ran while one was open for 6% -> 0% of each run, Pallas kernels for 0% -> 19%
where the time goes in v1:
time: 347 us; the launch traced here: 341 us
  starting transfers between devices  112 us (32%)
  waiting for transfers between devices  104 us (30%)
  Pallas kernels  92.3 us (27%)
  local copies, waits for them, and re-layouts  30.7 us (9%)
    ppermute x17, starting transfers between devices, swap_core(): return lax.ppermute(v, 'core', [(0, 1), (1, 0)])  50 us
    ppermute x28, waiting for transfers between devices, turn(): return lambda v: lax.ppermute(v, ('y', 'z', 'core'), pairs)  41.5 us
    unnamed x158, local copies, waits for them, and re-layouts  30.3 us
    ppermute x7, waiting for transfers between devices, swap_xh(): return lax.ppermute(v, 'xh', [(0, 1), (1, 0)])  26.3 us
    ppermute x10, waiting for transfers between devices, cross(): return lambda v: lax.ppermute(v, ('xl', 'xh', 'core'), pairs)  26.1 us
    ppermute x28, starting transfers between devices, turn(): return lambda v: lax.ppermute(v, ('y', 'z', 'core'), pairs)  25.4 us
    pallas_call x1, Pallas kernels, mlp(): pl.pallas_call(mlp_kernel, in_specs=[SCALARS] * 2 + whole(*h, *cot, gains...  22.9 us
    pallas_call x1, Pallas kernels, attention_back(): pl.pallas_call(attention_back_kernel, in_specs=[SCALARS] + whole(*a, *h,...  18.9 us
  transfers between devices with their start and end apart: 67, of which 30 were waited for; matrix products, arithmetic and copies ran while one was open for 0% of the time, Pallas kernels for 19%

profile of v1, /device:TPU:1, one launch (start us, length us, event | category | flops | bytes accessed | tf_op | source)
XLA Modules:
  0.0 341.5 jit_solution(14995229321409895540)
XLA Ops:
  20.2 5.9 %collective-permute-done.5.refs_2_ = bf16[1184,128]{1,0:T(8,128)(2,1)S(1)} collective-permute-done((bf16[1184,128]{1,0:T(8,128)(2,1)S(1)}, bf16[1184,128]{1,0:T(8,128)(2,1)S(1)}, u32[]{:S(2)}, u32[]{:S(2)}) %collective-permute-start.5) | collective-permute-done | bytes 303136 | tf_op jit(solution)/shard_map/ppermute | solution.py:38
  35.3 6.0 %collective-permute-start = (bf16[512,512]{1,0:T(8,128)(2,1)S(1)}, bf16[512,512]{1,0:T(8,128)(2,1)}, u32[]{:S(2)}, u32[]{:S(2)}) collective-permute-start(bf16[512,512]{1,0:T(8,128)(2,1)S(1)} %get-tuple-element.96.x0.refs_27_.x), channel_id=1, source_target_pairs={{0,1},{1,0},{2,3},{3,2},{4,5},{5,4},{6,7},{7,6},{8,9},{9,8},{10,11... | collective-permute-start | bytes 1572872 | tf_op jit(solution)/shard_map/ppermute | solution.py:50
  51.7 6.7 %collective-permute-start.2 = (bf16[512,512]{1,0:T(8,128)(2,1)}, bf16[512,512]{1,0:T(8,128)(2,1)}, u32[]{:S(2)}, u32[]{:S(2)}) collective-permute-start(bf16[512,512]{1,0:T(8,128)(2,1)} %collective-permute-done.1.x2.refs_29_), channel_id=1, source_target_pairs={{0,1},{1,0},{2,3},{3,2},{4,5},{5,4},{6,7},{7,6},{8,9},{9,8},{10,11... | collective-permute-start | bytes 1572872 | tf_op jit(solution)/shard_map/ppermute | solution.py:50
  65.8 10.6 %shard_map.200 = (bf16[512,2048]{1,0:T(8,128)(2,1)S(1)}, bf16[8,512,512]{2,1,0:T(8,128)(2,1)S(1)}, f32[512,1]{1,0:T(8,128)S(1)}, bf16[512,512]{1,0:T(8,128)(2,1)...) custom-call(s32[16]{0:T(128)S(1)} %reshape.53.table, ...), custom_call_target="tpu_custom_call" | custom-call | flops 16099999744 | tf_op jit(solution)/shard_map/pallas_call | solution.py:573
  80.0 6.9 %collective-permute-start.11 = (bf16[2,512,512]{2,1,0:T(8,128)(2,1)S(1)}, bf16[2,512,512]{2,1,0:T(8,128)(2,1)S(1)}, u32[]{:S(2)}, u32[]{:S(2)}) collective-permute-start(bf16[2,512,512]{2,1,0:T(8,128)(2,1)S(1)} %get-tuple-element.102), channel_id=1, source_target_pairs={{0,1},{1,0},{2,3},{3,2},{4,5},{5,4},{6,7},{7,6},{8,9},{9,8},{10,11... | collective-permute-start | bytes 3145736 | tf_op jit(solution)/shard_map/ppermute | solution.py:50
  92.3 8.2 %collective-permute-done.20.refs_8_ = bf16[512,512]{1,0:T(8,128)(2,1)S(1)} collective-permute-done((bf16[512,512]{1,0:T(8,128)(2,1)S(1)}, bf16[512,512]{1,0:T(8,128)(2,1)S(1)}, u32[]{:S(2)}, u32[]{:S(2)}) %collective-permute-start.20) | collective-permute-done | bytes 524320 | tf_op jit(solution)/shard_map/ppermute | solution.py:46
  103.4 9.4 %collective-permute-start.24 = (bf16[512,512]{1,0:T(8,128)(2,1)S(1)}, bf16[512,512]{1,0:T(8,128)(2,1)S(1)}, u32[]{:S(2)}, u32[]{:S(2)}) collective-permute-start(bf16[512,512]{1,0:T(8,128)(2,1)S(1)} %copy-done.29), channel_id=1, source_target_pairs={{0,1},{1,0},{2,3},{3,2},{4,5},{5,4},{6,7},{7,6},{8,9},{9,8},{10,11... | collective-permute-start | bytes 1572872 | tf_op jit(solution)/shard_map/ppermute | solution.py:50
  122.8 5.6 %collective-permute-start.17 = (bf16[512,512]{1,0:T(8,128)(2,1)S(1)}, bf16[512,512]{1,0:T(8,128)(2,1)S(1)}, u32[]{:S(2)}, u32[]{:S(2)}) collective-permute-start(bf16[512,512]{1,0:T(8,128)(2,1)S(1)} %get-tuple-element.182.refs_4_), channel_id=1, source_target_pairs={{0,1},{1,0},{2,3},{3,2},{4,5},{5,4},{6,7},{7,6},{8,9},{9,8},{10,11... | collective-permute-start | bytes 1572872 | tf_op jit(solution)/shard_map/ppermute | solution.py:50
  130.1 5.3 %collective-permute-done.15.refs_2_ = bf16[512,512]{1,0:T(8,128)(2,1)S(1)} collective-permute-done((bf16[512,512]{1,0:T(8,128)(2,1)S(1)}, bf16[512,512]{1,0:T(8,128)(2,1)S(1)}, u32[]{:S(2)}, u32[]{:S(2)}) %collective-permute-start.15) | collective-permute-done | bytes 524320 | tf_op jit(solution)/shard_map/ppermute | solution.py:46
  137.1 3.9 %collective-permute-done.18.refs_6_ = bf16[512,512]{1,0:T(8,128)(2,1)S(1)} collective-permute-done((bf16[512,512]{1,0:T(8,128)(2,1)S(1)}, bf16[512,512]{1,0:T(8,128)(2,1)S(1)}, u32[]{:S(2)}, u32[]{:S(2)}) %collective-permute-start.18) | collective-permute-done | bytes 524320 | tf_op jit(solution)/shard_map/ppermute | solution.py:46
  141.0 3.9 %collective-permute-start.19 = (bf16[512,512]{1,0:T(8,128)(2,1)S(1)}, bf16[512,512]{1,0:T(8,128)(2,1)S(1)}, u32[]{:S(2)}, u32[]{:S(2)}) collective-permute-start(bf16[512,512]{1,0:T(8,128)(2,1)S(1)} %collective-permute-done.18.refs_6_), channel_id=1, source_target_pairs={{0,1},{1,0},{2,3},{3,2},{4,5},{5,4},{6,7},{7,6},{8,9},{9,8},{10,11... | collective-permute-start | bytes 1572872 | tf_op jit(solution)/shard_map/ppermute | solution.py:50
  146.5 22.9 %shard_map.205 = (f32[512,1]{1,0:T(8,128)S(1)}, bf16[1024,2048]{1,0:T(8,128)(2,1)}, bf16[1024,2048]{1,0:T(8,128)(2,1)}, bf16[704,1024]{1,0:T(8,128)(2,1)S(1)}, b...) custom-call(s32[16]{0:T(128)S(1)} %reshape.53.table, s32[7]{0:T(128)S(1)} %stack.31.where, ...), custom_call_target="tpu_custom_call" | custom-call | flops 34500001792 | tf_op jit(solution)/shard_map/pallas_call | solution.py:655
  170.5 4.0 %collective-permute-done.35.b = bf16[4,512,512]{2,1,0:T(8,128)(2,1)S(1)} collective-permute-done((bf16[4,512,512]{2,1,0:T(8,128)(2,1)}, bf16[4,512,512]{2,1,0:T(8,128)(2,1)S(1)}, u32[]{:S(2)}, u32[]{:S(2)}) %collective-permute-start.35) | collective-permute-done | bytes 2097184 | tf_op jit(solution)/shard_map/ppermute | solution.py:50
  181.9 13.8 %shard_map.212 = (bf16[2,2112,128]{2,1,0:T(8,128)(2,1)S(1)}, bf16[2,2112,128]{2,1,0:T(8,128)(2,1)S(1)}, bf16[4,2112,128]{2,1,0:T(8,128)(2,1)S(1)}, bf16[4,2112,1...) custom-call(s32[16]{0:T(128)S(1)} %reshape.53.table, bf16[1408,1024]{1,0:T(8,128)(2,1)S(1)} %copy-done.68, ...), custom_call_target="tpu_custom_call" | custom-call | flops 17250000896 | tf_op jit(solution)/shard_map/pallas_call | solution.py:743
  195.7 7.7 %collective-permute-done.38.d = bf16[512,512]{1,0:T(8,128)(2,1)S(1)} collective-permute-done((bf16[512,512]{1,0:T(8,128)(2,1)S(1)}, bf16[512,512]{1,0:T(8,128)(2,1)S(1)}, u32[]{:S(2)}, u32[]{:S(2)}) %collective-permute-start.38) | collective-permute-done | bytes 524320 | tf_op jit(solution)/shard_map/ppermute | solution.py:54
  207.4 6.3 %shard_map.208 = (bf16[4,512,512]{2,1,0:T(8,128)(2,1)S(1)}, bf16[4,512,512]{2,1,0:T(8,128)(2,1)}) custom-call(s32[16]{0:T(128)S(1)} %reshape.53.table, s32[7]{0:T(128)S(1)} %stack.31.where, bf16[704,1024]{1,0:T(8,128)(2,1)S(1)} %copy-done.65, bf16[4,2112,128]{2,1,0:T(8,128)(2,1)S(1)} %copy-done.12, bf16[4,2112,128]{2,1,0:T(8,128)(2,1)S(1)} %copy-done.14, ...), custom_call_target="tpu_custom_call" | custom-call | flops 8049999872 | tf_op jit(solution)/shard_map/pallas_call | solution.py:691
  213.7 4.9 %collective-permute-done.39.refs_0_ = bf16[512,512]{1,0:T(8,128)(2,1)S(1)} collective-permute-done((bf16[512,512]{1,0:T(8,128)(2,1)S(1)}, bf16[512,512]{1,0:T(8,128)(2,1)S(1)}, u32[]{:S(2)}, u32[]{:S(2)}) %collective-permute-start.39) | collective-permute-done | bytes 524320 | tf_op jit(solution)/shard_map/ppermute | solution.py:54
  229.9 18.9 %shard_map.215 = (f32[512,512]{1,0:T(8,128)S(1)}, bf16[2,528,512]{2,1,0:T(8,128)(2,1)S(1)}, bf16[2,528,512]{2,1,0:T(8,128)(2,1)S(1)}, bf16[2,1152,128]{2,1,0:T(8...) custom-call(s32[16]{0:T(128)S(1)} %reshape.53.table, ...), custom_call_target="tpu_custom_call" | custom-call | flops 25300000768 | tf_op jit(solution)/shard_map/pallas_call | solution.py:841
  251.5 4.9 %collective-permute-start.48 = (bf16[2,528,512]{2,1,0:T(8,128)(2,1)S(1)}, bf16[2,528,512]{2,1,0:T(8,128)(2,1)S(1)}, u32[]{:S(2)}, u32[]{:S(2)}) collective-permute-start(bf16[2,528,512]{2,1,0:T(8,128)(2,1)S(1)} %get-tuple-element.148), channel_id=1, source_target_pairs={{0,1},{1,0},{2,3},{3,2},{4,5},{5,4},{6,7},{7,6},{8,9},{9,8},{10,11... | collective-permute-start | bytes 3244040 | tf_op jit(solution)/shard_map/ppermute | solution.py:50
  274.2 8.5 %collective-permute-done.60.refs_1_ = bf16[2112,128]{1,0:T(8,128)(2,1)S(1)} collective-permute-done((bf16[2112,128]{1,0:T(8,128)(2,1)S(1)}, bf16[2112,128]{1,0:T(8,128)(2,1)S(1)}, u32[]{:S(2)}, u32[]{:S(2)}) %collective-permute-start.60) | collective-permute-done | bytes 540704 | tf_op jit(solution)/shard_map/ppermute | solution.py:38
  284.0 10.6 %collective-permute-done.61.refs_2_ = bf16[2112,128]{1,0:T(8,128)(2,1)S(1)} collective-permute-done((bf16[2112,128]{1,0:T(8,128)(2,1)S(1)}, bf16[2112,128]{1,0:T(8,128)(2,1)S(1)}, u32[]{:S(2)}, u32[]{:S(2)}) %collective-permute-start.61) | collective-permute-done | bytes 540704 | tf_op jit(solution)/shard_map/ppermute | solution.py:38
  304.3 3.4 %collective-permute-start.58 = (bf16[1152,128]{1,0:T(8,128)(2,1)S(1)}, bf16[1152,128]{1,0:T(8,128)(2,1)S(1)}, u32[]{:S(2)}, u32[]{:S(2)}) collective-permute-start(bf16[1152,128]{1,0:T(8,128)(2,1)S(1)} %get-tuple-element.166), channel_id=1, source_target_pairs={{0,12},{1,97},{4,8},{5,101},{8,4},{9,105},{12,0},{13,109},{32,44},... | collective-permute-start | bytes 884744 | tf_op jit(solution)/shard_map/ppermute | solution.py:38
  307.8 8.3 %collective-permute-done.43.m3 = bf16[512,512]{1,0:T(8,128)(2,1)S(1)} collective-permute-done((bf16[512,512]{1,0:T(8,128)(2,1)S(1)}, bf16[512,512]{1,0:T(8,128)(2,1)S(1)}, u32[]{:S(2)}, u32[]{:S(2)}) %collective-permute-start.43) | collective-permute-done | bytes 524320 | tf_op jit(solution)/shard_map/ppermute | solution.py:54
  326.5 10.2 %collective-permute-start.66 = (f32[1,128]{1,0:T(1,128)S(1)}, f32[1,128]{1,0:T(1,128)S(1)}, u32[]{:S(2)}, u32[]{:S(2)}) collective-permute-start(f32[1,128]{1,0:T(1,128)S(1)} %maximum_bitcast_fusion), channel_id=1, source_target_pairs={{0,3},{1,2},{2,1},{3,0},{4,7},{5,6},{6,5},{7,4},{8,11},{9,10},{10,... | collective-permute-start | bytes 1544 | tf_op jit(solution)/shard_map/ppermute | solution.py:58
  (310 shorter events, 143.2 us)
Async XLA Ops:
  32.5 19.2 %collective-permute-start.1 = (bf16[512,512]{1,0:T(8,128)(2,1)S(1)}, bf16[512,512]{1,0:T(8,128)(2,1)}, u32[]{:S(2)}, u32[]{:S(2)}) collective-permute-start(bf16[512,512]{1,0:T(8,128)(2,1)S(1)} %get-tuple-element.96.x0.refs_27_.x), channel_id=1, source_target_pairs={{0,2},{2,0},{1,3},{3,1},{4,6},{6,4},{5,7},{7,5},{8,10},{10,8},{9,1... | collective-permute-start | bytes 1572872 | tf_op jit(solution)/shard_map/ppermute | solution.py:54
  35.3 27.6 %collective-permute-start = (bf16[512,512]{1,0:T(8,128)(2,1)S(1)}, bf16[512,512]{1,0:T(8,128)(2,1)}, u32[]{:S(2)}, u32[]{:S(2)}) collective-permute-start(bf16[512,512]{1,0:T(8,128)(2,1)S(1)} %get-tuple-element.96.x0.refs_27_.x), channel_id=1, source_target_pairs={{0,1},{1,0},{2,3},{3,2},{4,5},{5,4},{6,7},{7,6},{8,9},{9,8},{10,11... | collective-permute-start | bytes 1572872 | tf_op jit(solution)/shard_map/ppermute | solution.py:50
  41.3 17.5 %collective-permute-start.27 = (bf16[1056,128]{1,0:T(8,128)(2,1)S(1)}, bf16[1056,128]{1,0:T(8,128)(2,1)}, u32[]{:S(2)}, u32[]{:S(2)}) collective-permute-start(bf16[1056,128]{1,0:T(8,128)(2,1)S(1)} %get-tuple-element.98.refs_0_.refs_4_), channel_id=1, source_target_pairs={{0,16},{16,0},{1,17},{17,1},{2,18},{18,2},{3,19},{19,3},{4,20},{20... | collective-permute-start | bytes 811016 | tf_op jit(solution)/shard_map/ppermute | solution.py:62
  80.0 40.5 %collective-permute-start.31 = (bf16[4,2112,128]{2,1,0:T(8,128)(2,1)S(1)}, bf16[4,2112,128]{2,1,0:T(8,128)(2,1)S(1)}, u32[]{:S(2)}, u32[]{:S(2)}) collective-permute-start(bf16[4,2112,128]{2,1,0:T(8,128)(2,1)S(1)} %shard_map.203.refs_17_.refs_0_), channel_id=1, source_target_pairs={{0,32},{1,5},{4,36},{5,1},{8,40},{9,13},{12,44},{13,9},{32,0},{33,... | collective-permute-start | bytes 6488072 | tf_op jit(solution)/shard_map/ppermute | solution.py:38
  80.0 40.6 %collective-permute-start.32 = (bf16[4,2112,128]{2,1,0:T(8,128)(2,1)S(1)}, bf16[4,2112,128]{2,1,0:T(8,128)(2,1)S(1)}, u32[]{:S(2)}, u32[]{:S(2)}) collective-permute-start(bf16[4,2112,128]{2,1,0:T(8,128)(2,1)S(1)} %shard_map.203.refs_17_.refs_0_), channel_id=1, source_target_pairs={{0,96},{1,13},{4,100},{5,9},{8,104},{9,5},{12,108},{13,1},{32,64},... | collective-permute-start | bytes 6488072 | tf_op jit(solution)/shard_map/ppermute | solution.py:38
  89.6 24.6 %collective-permute-start.12 = (bf16[512,512]{1,0:T(8,128)(2,1)S(1)}, bf16[512,512]{1,0:T(8,128)(2,1)S(1)}, u32[]{:S(2)}, u32[]{:S(2)}) collective-permute-start(bf16[512,512]{1,0:T(8,128)(2,1)S(1)} %get-tuple-element.104), channel_id=1, source_target_pairs={{0,2},{2,0},{1,3},{3,1},{4,6},{6,4},{5,7},{7,5},{8,10},{10,8},{9,1... | collective-permute-start | bytes 1572872 | tf_op jit(solution)/shard_map/ppermute | solution.py:54
  100.5 17.8 %collective-permute-start.25 = (bf16[512,512]{1,0:T(8,128)(2,1)S(1)}, bf16[512,512]{1,0:T(8,128)(2,1)S(1)}, u32[]{:S(2)}, u32[]{:S(2)}) collective-permute-start(bf16[512,512]{1,0:T(8,128)(2,1)S(1)} %collective-permute-done.20.refs_8_), channel_id=1, source_target_pairs={{0,18},{1,17},{2,16},{3,19},{16,2},{17,1},{18,0},{19,3},{4,22},{5,... | collective-permute-start | bytes 1572872 | tf_op jit(solution)/shard_map/ppermute | solution.py:46
  103.4 19.1 %collective-permute-start.24 = (bf16[512,512]{1,0:T(8,128)(2,1)S(1)}, bf16[512,512]{1,0:T(8,128)(2,1)S(1)}, u32[]{:S(2)}, u32[]{:S(2)}) collective-permute-start(bf16[512,512]{1,0:T(8,128)(2,1)S(1)} %copy-done.29), channel_id=1, source_target_pairs={{0,1},{1,0},{2,3},{3,2},{4,5},{5,4},{6,7},{7,6},{8,9},{9,8},{10,11... | collective-permute-start | bytes 1572872 | tf_op jit(solution)/shard_map/ppermute | solution.py:50
  122.5 24.0 %collective-permute-start.33 = (bf16[2,2112,128]{2,1,0:T(8,128)(2,1)S(1)}, bf16[2,2112,128]{2,1,0:T(8,128)(2,1)S(1)}, u32[]{:S(2)}, u32[]{:S(2)}) collective-permute-start(bf16[2,2112,128]{2,1,0:T(8,128)(2,1)S(1)} %get-tuple-element.109), channel_id=1, source_target_pairs={{0,96},{1,13},{4,100},{5,9},{8,104},{9,5},{12,108},{13,1},{32,64},... | collective-permute-start | bytes 3244040 | tf_op jit(solution)/shard_map/ppermute | solution.py:38
  122.5 24.0 %collective-permute-start.34 = (bf16[2,2112,128]{2,1,0:T(8,128)(2,1)S(1)}, bf16[2,2112,128]{2,1,0:T(8,128)(2,1)S(1)}, u32[]{:S(2)}, u32[]{:S(2)}) collective-permute-start(bf16[2,2112,128]{2,1,0:T(8,128)(2,1)S(1)} %get-tuple-element.110), channel_id=1, source_target_pairs={{0,32},{1,5},{4,36},{5,1},{8,40},{9,13},{12,44},{13,9},{32,0},{33,... | collective-permute-start | bytes 3244040 | tf_op jit(solution)/shard_map/ppermute | solution.py:38
  176.6 19.1 %collective-permute-start.36 = (bf16[512,512]{1,0:T(8,128)(2,1)S(1)}, bf16[512,512]{1,0:T(8,128)(2,1)S(1)}, u32[]{:S(2)}, u32[]{:S(2)}) collective-permute-start(bf16[512,512]{1,0:T(8,128)(2,1)S(1)} %get-tuple-element.115.refs_0_), channel_id=1, source_target_pairs={{0,16},{1,19},{2,18},{3,17},{16,0},{17,3},{18,2},{19,1},{4,20},{5,... | collective-permute-start | bytes 1572872 | tf_op jit(solution)/shard_map/ppermute | solution.py:46
  178.0 17.7 %collective-permute-start.37 = (bf16[512,512]{1,0:T(8,128)(2,1)S(1)}, bf16[512,512]{1,0:T(8,128)(2,1)S(1)}, u32[]{:S(2)}, u32[]{:S(2)}) collective-permute-start(bf16[512,512]{1,0:T(8,128)(2,1)S(1)} %get-tuple-element.116), channel_id=1, source_target_pairs={{0,18},{1,17},{2,16},{3,19},{16,2},{17,1},{18,0},{19,3},{4,22},{5,... | collective-permute-start | bytes 1572872 | tf_op jit(solution)/shard_map/ppermute | solution.py:46
  178.0 25.4 %collective-permute-start.38 = (bf16[512,512]{1,0:T(8,128)(2,1)S(1)}, bf16[512,512]{1,0:T(8,128)(2,1)S(1)}, u32[]{:S(2)}, u32[]{:S(2)}) collective-permute-start(bf16[512,512]{1,0:T(8,128)(2,1)S(1)} %get-tuple-element.117), channel_id=1, source_target_pairs={{0,2},{2,0},{1,3},{3,1},{4,6},{6,4},{5,7},{7,5},{8,10},{10,8},{9,1... | collective-permute-start | bytes 1572872 | tf_op jit(solution)/shard_map/ppermute | solution.py:54
  204.0 17.4 %collective-permute-start.44 = (bf16[512,512]{1,0:T(8,128)(2,1)S(1)}, bf16[512,512]{1,0:T(8,128)(2,1)S(1)}, u32[]{:S(2)}, u32[]{:S(2)}) collective-permute-start(bf16[512,512]{1,0:T(8,128)(2,1)S(1)} %shard_map.207.refs_5_.refs_0_), channel_id=1, source_target_pairs={{0,1},{1,0},{2,3},{3,2},{4,5},{5,4},{6,7},{7,6},{8,9},{9,8},{10,11... | collective-permute-start | bytes 1572872 | tf_op jit(solution)/shard_map/ppermute | solution.py:50
  220.7 38.5 %collective-permute-start.52 = (bf16[4,2112,128]{2,1,0:T(8,128)(2,1)S(1)}, bf16[4,2112,128]{2,1,0:T(8,128)(2,1)}, u32[]{:S(2)}, u32[]{:S(2)}) collective-permute-start(bf16[4,2112,128]{2,1,0:T(8,128)(2,1)S(1)} %get-tuple-element.145.refs_32_), channel_id=1, source_target_pairs={{0,32},{1,5},{4,36},{5,1},{8,40},{9,13},{12,44},{13,9},{32,0},{33,... | collective-permute-start | bytes 6488072 | tf_op jit(solution)/shard_map/ppermute | solution.py:38
  220.8 41.3 %collective-permute-start.53 = (bf16[4,2112,128]{2,1,0:T(8,128)(2,1)S(1)}, bf16[4,2112,128]{2,1,0:T(8,128)(2,1)}, u32[]{:S(2)}, u32[]{:S(2)}) collective-permute-start(bf16[4,2112,128]{2,1,0:T(8,128)(2,1)S(1)} %get-tuple-element.157), channel_id=1, source_target_pairs={{0,96},{1,13},{4,100},{5,9},{8,104},{9,5},{12,108},{13,1},{32,64},... | collective-permute-start | bytes 6488072 | tf_op jit(solution)/shard_map/ppermute | solution.py:38
  269.6 28.8 %collective-permute-start.54 = (bf16[4,1152,128]{2,1,0:T(8,128)(2,1)S(1)}, bf16[4,1152,128]{2,1,0:T(8,128)(2,1)S(1)}, u32[]{:S(2)}, u32[]{:S(2)}) collective-permute-start(bf16[4,1152,128]{2,1,0:T(8,128)(2,1)S(1)} %get-tuple-element.159.refs_4_), channel_id=1, source_target_pairs={{0,32},{1,5},{4,36},{5,1},{8,40},{9,13},{12,44},{13,9},{32,0},{33,... | collective-permute-start | bytes 3538952 | tf_op jit(solution)/shard_map/ppermute | solution.py:38
  269.7 29.5 %collective-permute-start.55 = (bf16[4,1152,128]{2,1,0:T(8,128)(2,1)S(1)}, bf16[4,1152,128]{2,1,0:T(8,128)(2,1)S(1)}, u32[]{:S(2)}, u32[]{:S(2)}) collective-permute-start(bf16[4,1152,128]{2,1,0:T(8,128)(2,1)S(1)} %get-tuple-element.160), channel_id=1, source_target_pairs={{0,96},{1,13},{4,100},{5,9},{8,104},{9,5},{12,108},{13,1},{32,64},... | collective-permute-start | bytes 3538952 | tf_op jit(solution)/shard_map/ppermute | solution.py:38
  270.9 23.6 %collective-permute-start.61 = (bf16[2112,128]{1,0:T(8,128)(2,1)S(1)}, bf16[2112,128]{1,0:T(8,128)(2,1)S(1)}, u32[]{:S(2)}, u32[]{:S(2)}) collective-permute-start(bf16[2112,128]{1,0:T(8,128)(2,1)S(1)} %get-tuple-element.173), channel_id=1, source_target_pairs={{0,8},{1,65},{4,12},{5,69},{8,0},{9,73},{12,4},{13,77},{32,40},{33... | collective-permute-start | bytes 1622024 | tf_op jit(solution)/shard_map/ppermute | solution.py:38
  273.3 23.0 %collective-permute-start.62 = (bf16[2112,128]{1,0:T(8,128)(2,1)S(1)}, bf16[2112,128]{1,0:T(8,128)(2,1)S(1)}, u32[]{:S(2)}, u32[]{:S(2)}) collective-permute-start(bf16[2112,128]{1,0:T(8,128)(2,1)S(1)} %get-tuple-element.174), channel_id=1, source_target_pairs={{0,12},{1,97},{4,8},{5,101},{8,4},{9,105},{12,0},{13,109},{32,44},... | collective-permute-start | bytes 1622024 | tf_op jit(solution)/shard_map/ppermute | solution.py:38
  282.7 18.6 %collective-permute-start.41 = (bf16[512,512]{1,0:T(8,128)(2,1)S(1)}, bf16[512,512]{1,0:T(8,128)(2,1)S(1)}, u32[]{:S(2)}, u32[]{:S(2)}) collective-permute-start(bf16[512,512]{1,0:T(8,128)(2,1)S(1)} %get-tuple-element.123), channel_id=1, source_target_pairs={{0,16},{1,19},{2,18},{3,17},{16,0},{17,3},{18,2},{19,1},{4,20},{5,... | collective-permute-start | bytes 1572872 | tf_op jit(solution)/shard_map/ppermute | solution.py:46
  296.4 19.7 %collective-permute-start.43 = (bf16[512,512]{1,0:T(8,128)(2,1)S(1)}, bf16[512,512]{1,0:T(8,128)(2,1)S(1)}, u32[]{:S(2)}, u32[]{:S(2)}) collective-permute-start(bf16[512,512]{1,0:T(8,128)(2,1)S(1)} %get-tuple-element.125), channel_id=1, source_target_pairs={{0,2},{2,0},{1,3},{3,1},{4,6},{6,4},{5,7},{7,5},{8,10},{10,8},{9,1... | collective-permute-start | bytes 1572872 | tf_op jit(solution)/shard_map/ppermute | solution.py:54
  298.4 22.3 %collective-permute-start.63 = (bf16[1056,128]{1,0:T(8,128)(2,1)S(1)}, bf16[1056,128]{1,0:T(8,128)(2,1)S(1)}, u32[]{:S(2)}, u32[]{:S(2)}) collective-permute-start(bf16[1056,128]{1,0:T(8,128)(2,1)S(1)} %get-tuple-element.176), channel_id=1, source_target_pairs={{0,16},{16,0},{1,17},{17,1},{2,18},{18,2},{3,19},{19,3},{4,20},{20... | collective-permute-start | bytes 811016 | tf_op jit(solution)/shard_map/ppermute | solution.py:62
  299.6 18.7 %collective-permute-start.56 = (bf16[1152,128]{1,0:T(8,128)(2,1)S(1)}, bf16[1152,128]{1,0:T(8,128)(2,1)S(1)}, u32[]{:S(2)}, u32[]{:S(2)}) collective-permute-start(bf16[1152,128]{1,0:T(8,128)(2,1)S(1)} %get-tuple-element.164), channel_id=1, source_target_pairs={{0,4},{1,33},{4,0},{5,37},{8,12},{9,41},{12,8},{13,45},{32,36},{33... | collective-permute-start | bytes 884744 | tf_op jit(solution)/shard_map/ppermute | solution.py:38
  (122 other events, 1091.8 us)

commit v2 on v1

--- a/solution.py
+++ b/solution.py
@@ -117,8 +117,16 @@
     return pl.BlockSpec(shape, index if index is not None else (lambda *_: zeros))
 
 
+def held_by(arrays):
+    return [a[0] if isinstance(a, tuple) else a for a in arrays]
+
+
 def whole(*arrays):
-    return [spec(a.shape) for a in arrays]
+    return [spec(a.shape) for a in held_by(arrays)]
+
+
+def views(refs, k):
+    return [ref.at[k] if len(ref.shape) == 3 else ref for ref in refs]
 
 
 def out(*shape, dtype=BF16):
@@ -261,6 +269,42 @@
         out_shape=shapes,
         compiler_params=params(),
         cost_estimate=cost(2),
+    )(keep, swap_core(send))
+
+
+def add_two_kernel(a, b, total_o):
+    total_o[...] = narrow(wide(a[...]) + wide(b[1]))
+
+
+def add_two(a, b):
+    return pl.pallas_call(
+        add_two_kernel,
+        in_specs=whole(a, b),
+        out_specs=spec(a.shape),
+        out_shape=out(*a.shape),
+        compiler_params=params(),
+        cost_estimate=cost(1),
+    )(*held_by((a, b)))
+
+
+def add_paired_kernel(a, b, pair_o, second_o, own_o):
+    total = lambda k: narrow(wide(a[k]) + wide(b[k]))
+    pair_o[0] = total(0)
+    second_o[...] = total(1)
+    own_o[...] = total(2)
+    pair_o[1] = total(3)
+
+
+def add_cores_paired(keep, send):
+    block = out(*keep.shape[1:])
+    shapes = (out(2, *keep.shape[1:]), block, block)
+    return pl.pallas_call(
+        add_paired_kernel,
+        in_specs=whole(keep, send),
+        out_specs=tuple(whole(*shapes)),
+        out_shape=shapes,
+        compiler_params=params(),
+        cost_estimate=cost(3),
     )(keep, swap_core(send))
 
 
@@ -488,15 +532,15 @@
     return jnp.concatenate([a * cos + b * sin, b * cos - a * sin], 0)
 
 
-def bundle_kernel(*refs):
-    for k in range(4):
+def bundle_kernel(*refs, count):
+    for k in range(count):
         refs[-1][k] = refs[k][...]
 
 
 def bundle(parts, after):
-    shape = out(4, *parts[0].shape)
-    return pl.pallas_call(
-        bundle_kernel,
+    shape = out(len(parts), *parts[0].shape)
+    return pl.pallas_call(
+        functools.partial(bundle_kernel, count=len(parts)),
         in_specs=whole(*parts) + [ANYWHERE] * len(after),
         out_specs=spec(shape.shape),
         out_shape=shape,
@@ -595,7 +639,8 @@
 
 
 def mlp_kernel(table, where, *refs):
-    h_in, cot_in, gains, blocks, refs = refs[:8], refs[8:16], refs[16], refs[17:22], refs[22:]
+    h_in, cot_in = (views(refs[k : k + 4], 0) + views(refs[k + 4 : k + 8], 1) for k in (0, 8))
+    gains, blocks, refs = refs[16], refs[17:22], refs[22:]
     r_o, n_o, cot_o, act_o, dgu_o, keep_o, send_o = refs[:7]
     w, wd, h, cot, n, act, dgu, chunk, sems, wd_sems, saves = refs[7:]
     copies = fetch(table, blocks, w, sems, 0)
@@ -672,7 +717,7 @@
         ],
         compiler_params=params(42),
         cost_estimate=cost(30),
-    )(table, where, *h, *cot, gains, *blocks)
+    )(table, where, *held_by((*h, *cot)), gains, *blocks)
 
 
 def down_kernel(table, where, act, *refs):
@@ -762,7 +807,8 @@
 
 
 def attention_back_kernel(table, *refs):
-    a_in, h_in, cot_in, (r, gains), refs = refs[:4], refs[4:8], refs[8:12], refs[12:14], refs[14:]
+    a_in, h_in, cot_in = refs[:4], views(refs[4:8], 1), views(refs[8:12], 1)
+    (r, gains), refs = refs[12:14], refs[14:]
     (q, k, v, o, cos, sin), (n_in, p_in), blocks, refs = refs[:6], refs[6:8], refs[8:13], refs[13:]
     x_in, refs = refs[:4], refs[4:]
     (r_one, *_), refs = refs[:1], refs[-27:]
@@ -870,12 +916,12 @@
         ],
         compiler_params=params(34),
         cost_estimate=cost(22),
-    )(table, *a, *h, *cot, r, gains, q, k, v, o, cos, sin, n, p, *blocks, *x, r_one, *after)
-
-
-def outputs_kernel(h, m0, m1, m2, m3, dh, c0, c1, x, r, gains, *refs):
+    )(table, *held_by((*a, *h, *cot)), r, gains, q, k, v, o, cos, sin, n, p, *blocks, *x, r_one, *after)
+
+
+def outputs_kernel(h, m0, m1, m2, dh, c0, c1, x, r, gains, *refs):
     mixed_o, grad_o = refs[-2:]
-    m = wide(m0[...]) + wide(m1[...]) + wide(m2[...]) + wide(m3[...])
+    m = wide(m0[...]) + wide(m1[0]) + wide(m2[...])
     mixed_o[...] = narrow(to_natural(h[...] + m))
     total = wide(c0[...]) + wide(c1[...])
     stat = total[SEQ:].T[:, :1] * (1.0 / MODEL)
@@ -895,7 +941,7 @@
         out_shape=shapes,
         compiler_params=params(),
         cost_estimate=cost(5),
-    )(*args, gains, *after)
+    )(*held_by(args), gains, *after)
 
 
 def spread_eight(own, opposite, first, second):
@@ -911,6 +957,13 @@
     first, second = cross(False), cross(True)
     a, b = first(v), second(v)
     return (a, swap_core(a), b, swap_core(b)), second(a)
+
+
+def gather_eight(v):
+    a = cross(False)(v)
+    both = cross(True)(bundle((v, a), ()))
+    turned = swap_core(both)
+    return (a, swap_core(a), (both, 0), (turned, 0)), (v, swap_core(v), (both, 1), (turned, 1))
 
 
 def gather_own(v, opposite):
@@ -960,8 +1013,7 @@
     mlp_shard = merge(
         other_at, mlp_keep, swap_xl(mlp_pack), (attn_blocks[1], attn_blocks[4])
     )
-    cot_other, opposite = gather_other(cot_own)
-    cot_self = gather_own(cot_own, opposite)
+    cot_other, cot_self = gather_eight(cot_own)
 
     frequency = jnp.exp(jnp.arange(HALF).astype(F32) * (-2.0 * math.log(10000.0) / HEAD))
     angles = frequency[:, None] * position.astype(F32)[None, :]
@@ -987,8 +1039,9 @@
     keep, send = tie((keep, send), opposite)
     d_normed_all = gather_own(d_normed_two, opposite)
     mlp_terms = reduce_start(mlp_terms, ())
-    sum_out = add_cores(keep, send)
-    mlp_out = spread_eight(sum_out[2], sum_out[3], sum_out[0], sum_out[1])
+    away, second, own = add_cores_paired(keep, send)
+    passed = cross(False)(away)
+    mlp_out = own, (passed, 0), cross(True)(add_two(second, (passed, 1)))
     d_resid, keep, send, *attn_terms = attention_back(
         table,
         d_normed_all,

time: 347 us -> 323 us (0.931)
  waiting for transfers between devices: 104 us -> 91.7 us
  starting transfers between devices: 112 us -> 104 us
  local copies, waits for them, and re-layouts: 30.7 us -> 23.1 us
    ppermute x7 -> x6, waiting for transfers between devices: 26.3 us -> 13.7 us  [swap_xh(): return lax.ppermute(v, 'xh', [(0, 1), (1, 0)])]
    ppermute x17 -> x16, starting transfers between devices: 50 us -> 39 us  [swap_core(): return lax.ppermute(v, 'core', [(0, 1), (1, 0)])]
    unnamed x158 -> x156, local copies, waits for them, and re-layouts: 30.3 us -> 22.8 us
    ppermute x10 -> x9, starting transfers between devices: 8.71 us -> 13.2 us  [cross(): return lambda v: lax.ppermute(v, ('xl', 'xh', 'core'), pairs)]
    ppermute x28, starting transfers between devices: 25.4 us -> 29.3 us  [turn(): return lambda v: lax.ppermute(v, ('y', 'z', 'core'), pairs)]
    ppermute x1, starting transfers between devices: 10.2 us -> 6.52 us  [swap_both(): return lax.ppermute(v, ('xh', 'core'), [(i, i ^ 3) for i in range(4)])]
    ppermute x10 -> x9, waiting for transfers between devices: 26.1 us -> 29.7 us  [cross(): return lambda v: lax.ppermute(v, ('xl', 'xh', 'core'), pairs)]
    ppermute x17 -> x16, waiting for transfers between devices: 7.19 us -> 5.57 us  [swap_core(): return lax.ppermute(v, 'core', [(0, 1), (1, 0)])]
  transfers between devices with their start and end apart: 67 -> 64, of which waited for: 30 -> 27; matrix products, arithmetic and copies ran while one was open for 0% -> 1% of each run, Pallas kernels for 19% -> 21%
where the time goes in v2:
time: 323 us; the launch traced here: 316 us
  starting transfers between devices  104 us (32%)
  Pallas kernels  93.9 us (29%)
  waiting for transfers between devices  91.7 us (28%)
  local copies, waits for them, and re-layouts  23.1 us (7%)
    ppermute x28, waiting for transfers between devices, turn(): return lambda v: lax.ppermute(v, ('y', 'z', 'core'), pairs)  40.1 us
    ppermute x16, starting transfers between devices, swap_core(): return lax.ppermute(v, 'core', [(0, 1), (1, 0)])  39 us
    ppermute x9, waiting for transfers between devices, cross(): return lambda v: lax.ppermute(v, ('xl', 'xh', 'core'), pairs)  29.7 us
    ppermute x28, starting transfers between devices, turn(): return lambda v: lax.ppermute(v, ('y', 'z', 'core'), pairs)  29.3 us
    pallas_call x1, Pallas kernels, mlp(): pl.pallas_call(mlp_kernel, in_specs=[SCALARS] * 2 + whole(*h, *cot, gains...  22.8 us
    unnamed x156, local copies, waits for them, and re-layouts  22.8 us
    pallas_call x1, Pallas kernels, attention_back(): pl.pallas_call(attention_back_kernel, in_specs=[SCALARS] + whole(*a, *h,...  19.1 us
    pallas_call x1, Pallas kernels, grads_mlp(): pl.pallas_call(grads_mlp_kernel, in_specs=[SCALARS] + [ANYWHERE] * (4 + l...  13.7 us
  transfers between devices with their start and end apart: 64, of which 27 were waited for; matrix products, arithmetic and copies ran while one was open for 1% of the time, Pallas kernels for 21%

profile of v2, /device:TPU:1, one launch (start us, length us, event | category | flops | bytes accessed | tf_op | source)
XLA Modules:
  0.0 316.3 jit_solution(146849450146985279)
XLA Ops:
  19.5 5.9 %collective-permute-done.5.refs_2_ = bf16[1184,128]{1,0:T(8,128)(2,1)S(1)} collective-permute-done((bf16[1184,128]{1,0:T(8,128)(2,1)S(1)}, bf16[1184,128]{1,0:T(8,128)(2,1)S(1)}, u32[]{:S(2)}, u32[]{:S(2)}) %collective-permute-start.5) | collective-permute-done | bytes 303136 | tf_op jit(solution)/shard_map/ppermute | solution.py:38
  34.6 6.0 %collective-permute-start = (bf16[512,512]{1,0:T(8,128)(2,1)S(1)}, bf16[512,512]{1,0:T(8,128)(2,1)}, u32[]{:S(2)}, u32[]{:S(2)}) collective-permute-start(bf16[512,512]{1,0:T(8,128)(2,1)S(1)} %get-tuple-element.95.x0.refs_27_.x), channel_id=1, source_target_pairs={{0,1},{1,0},{2,3},{3,2},{4,5},{5,4},{6,7},{7,6},{8,9},{9,8},{10,11... | collective-permute-start | bytes 1572872 | tf_op jit(solution)/shard_map/ppermute | solution.py:50
  40.9 3.2 collective-permute-done.7.a.refs_1_.refs_0_.refs_23_
  51.0 6.7 %collective-permute-start.2 = (bf16[512,512]{1,0:T(8,128)(2,1)}, bf16[512,512]{1,0:T(8,128)(2,1)}, u32[]{:S(2)}, u32[]{:S(2)}) collective-permute-start(bf16[512,512]{1,0:T(8,128)(2,1)} %collective-permute-done.1.x2.refs_29_), channel_id=1, source_target_pairs={{0,1},{1,0},{2,3},{3,2},{4,5},{5,4},{6,7},{7,6},{8,9},{9,8},{10,11... | collective-permute-start | bytes 1572872 | tf_op jit(solution)/shard_map/ppermute | solution.py:50
  67.5 10.6 %shard_map.200 = (bf16[512,2048]{1,0:T(8,128)(2,1)S(1)}, bf16[8,512,512]{2,1,0:T(8,128)(2,1)S(1)}, f32[512,1]{1,0:T(8,128)S(1)}, bf16[512,512]{1,0:T(8,128)(2,1)...) custom-call(s32[16]{0:T(128)S(1)} %reshape.53.table, ...), custom_call_target="tpu_custom_call" | custom-call | flops 16099999744 | tf_op jit(solution)/shard_map/pallas_call | solution.py:617
  86.1 4.7 %collective-permute-start.12 = (bf16[512,512]{1,0:T(8,128)(2,1)S(1)}, bf16[512,512]{1,0:T(8,128)(2,1)S(1)}, u32[]{:S(2)}, u32[]{:S(2)}) collective-permute-start(bf16[512,512]{1,0:T(8,128)(2,1)S(1)} %get-tuple-element.103), channel_id=1, source_target_pairs={{0,2},{2,0},{1,3},{3,1},{4,6},{6,4},{5,7},{7,5},{8,10},{10,8},{9,1... | collective-permute-start | bytes 1572872 | tf_op jit(solution)/shard_map/ppermute | solution.py:54
  90.7 14.4 %collective-permute-done.22.refs_10_.refs_14_ = bf16[2,512,512]{2,1,0:T(8,128)(2,1)S(1)} collective-permute-done((bf16[2,512,512]{2,1,0:T(8,128)(2,1)S(1)}, bf16[2,512,512]{2,1,0:T(8,128)(2,1)S(1)}, u32[]{:S(2)}, u32[]{:S(2)}) %collective-permute-start.22) | collective-permute-done | bytes 1048608 | tf_op jit(solution)/shard_map/ppermute | solution.py:46
  105.1 7.9 %collective-permute-start.23 = (bf16[2,512,512]{2,1,0:T(8,128)(2,1)S(1)}, bf16[2,512,512]{2,1,0:T(8,128)(2,1)S(1)}, u32[]{:S(2)}, u32[]{:S(2)}) collective-permute-start(bf16[2,512,512]{2,1,0:T(8,128)(2,1)S(1)} %collective-permute-done.22.refs_10_.refs_14_), channel_id=1, source_target_pairs={{0,1},{1,0},{2,3},{3,2},{4,5},{5,4},{6,7},{7,6},{8,9},{9,8},{10,11... | collective-permute-start | bytes 3145736 | tf_op jit(solution)/shard_map/ppermute | solution.py:50
  114.7 3.4 %collective-permute-start.13 = (bf16[512,512]{1,0:T(8,128)(2,1)S(1)}, bf16[512,512]{1,0:T(8,128)(2,1)S(1)}, u32[]{:S(2)}, u32[]{:S(2)}) collective-permute-start(bf16[512,512]{1,0:T(8,128)(2,1)S(1)} %get-tuple-element.180.refs_4_), channel_id=1, source_target_pairs={{0,16},{1,19},{2,18},{3,17},{16,0},{17,3},{18,2},{19,1},{4,20},{5,... | collective-permute-start | bytes 1572872 | tf_op jit(solution)/shard_map/ppermute | solution.py:46
  119.7 3.7 %collective-permute-start.17 = (bf16[512,512]{1,0:T(8,128)(2,1)S(1)}, bf16[512,512]{1,0:T(8,128)(2,1)S(1)}, u32[]{:S(2)}, u32[]{:S(2)}) collective-permute-start(bf16[512,512]{1,0:T(8,128)(2,1)S(1)} %get-tuple-element.180.refs_4_), channel_id=1, source_target_pairs={{0,1},{1,0},{2,3},{3,2},{4,5},{5,4},{6,7},{7,6},{8,9},{9,8},{10,11... | collective-permute-start | bytes 1572872 | tf_op jit(solution)/shard_map/ppermute | solution.py:50
  125.4 3.7 %collective-permute-done.15.refs_2_ = bf16[512,512]{1,0:T(8,128)(2,1)S(1)} collective-permute-done((bf16[512,512]{1,0:T(8,128)(2,1)S(1)}, bf16[512,512]{1,0:T(8,128)(2,1)S(1)}, u32[]{:S(2)}, u32[]{:S(2)}) %collective-permute-start.15) | collective-permute-done | bytes 524320 | tf_op jit(solution)/shard_map/ppermute | solution.py:46
  134.7 3.4 %collective-permute-start.19 = (bf16[512,512]{1,0:T(8,128)(2,1)S(1)}, bf16[512,512]{1,0:T(8,128)(2,1)S(1)}, u32[]{:S(2)}, u32[]{:S(2)}) collective-permute-start(bf16[512,512]{1,0:T(8,128)(2,1)S(1)} %collective-permute-done.18.refs_6_), channel_id=1, source_target_pairs={{0,1},{1,0},{2,3},{3,2},{4,5},{5,4},{6,7},{7,6},{8,9},{9,8},{10,11... | collective-permute-start | bytes 1572872 | tf_op jit(solution)/shard_map/ppermute | solution.py:50
  139.8 22.8 %shard_map.206 = (f32[512,1]{1,0:T(8,128)S(1)}, bf16[1024,2048]{1,0:T(8,128)(2,1)}, bf16[1024,2048]{1,0:T(8,128)(2,1)}, bf16[704,1024]{1,0:T(8,128)(2,1)S(1)}, b...) custom-call(s32[16]{0:T(128)S(1)} %reshape.53.table, s32[7]{0:T(128)S(1)} %stack.31.where, ...), custom_call_target="tpu_custom_call" | custom-call | flops 34500001792 | tf_op jit(solution)/shard_map/pallas_call | solution.py:700
  163.1 4.0 %collective-permute-done.33.b = bf16[4,512,512]{2,1,0:T(8,128)(2,1)S(1)} collective-permute-done((bf16[4,512,512]{2,1,0:T(8,128)(2,1)}, bf16[4,512,512]{2,1,0:T(8,128)(2,1)S(1)}, u32[]{:S(2)}, u32[]{:S(2)}) %collective-permute-start.33) | collective-permute-done | bytes 2097184 | tf_op jit(solution)/shard_map/ppermute | solution.py:50
  175.7 13.7 %shard_map.214 = (bf16[2,2112,128]{2,1,0:T(8,128)(2,1)S(1)}, bf16[2,2112,128]{2,1,0:T(8,128)(2,1)S(1)}, bf16[4,2112,128]{2,1,0:T(8,128)(2,1)S(1)}, bf16[4,2112,1...) custom-call(s32[16]{0:T(128)S(1)} %reshape.53.table, bf16[1408,1024]{1,0:T(8,128)(2,1)S(1)} %copy-done.63, ...), custom_call_target="tpu_custom_call" | custom-call | flops 17250000896 | tf_op jit(solution)/shard_map/pallas_call | solution.py:788
  189.5 7.1 %collective-permute-done.36.d = bf16[512,512]{1,0:T(8,128)(2,1)S(1)} collective-permute-done((bf16[512,512]{1,0:T(8,128)(2,1)S(1)}, bf16[512,512]{1,0:T(8,128)(2,1)S(1)}, u32[]{:S(2)}, u32[]{:S(2)}) %collective-permute-start.36) | collective-permute-done | bytes 524320 | tf_op jit(solution)/shard_map/ppermute | solution.py:54
  201.6 5.1 %shard_map.209 = (bf16[4,512,512]{2,1,0:T(8,128)(2,1)S(1)}, bf16[4,512,512]{2,1,0:T(8,128)(2,1)S(1)}) custom-call(s32[16]{0:T(128)S(1)} %reshape.53.table, s32[7]{0:T(128)S(1)} %stack.31.where, bf16[704,1024]{1,0:T(8,128)(2,1)S(1)} %copy-done.60, bf16[4,2112,128]{2,1,0:T(8,128)(2,1)S(1)} %copy-done.15, bf16[4,2112,128]{2,1,0:T(8,128)(2,1)S(1)} %copy-done.17, ...), custom_call_target="tpu_custom_call" | custom-call | flops 8049999872 | tf_op jit(solution)/shard_map/pallas_call | solution.py:736
  206.7 4.0 %collective-permute-done.37.refs_0_ = bf16[512,512]{1,0:T(8,128)(2,1)S(1)} collective-permute-done((bf16[512,512]{1,0:T(8,128)(2,1)S(1)}, bf16[512,512]{1,0:T(8,128)(2,1)S(1)}, u32[]{:S(2)}, u32[]{:S(2)}) %collective-permute-start.37) | collective-permute-done | bytes 524320 | tf_op jit(solution)/shard_map/ppermute | solution.py:54
  218.9 19.1 %shard_map.217 = (f32[512,512]{1,0:T(8,128)S(1)}, bf16[2,528,512]{2,1,0:T(8,128)(2,1)S(1)}, bf16[2,528,512]{2,1,0:T(8,128)(2,1)S(1)}, bf16[2,1152,128]{2,1,0:T(8...) custom-call(s32[16]{0:T(128)S(1)} %reshape.53.table, ...), custom_call_target="tpu_custom_call" | custom-call | flops 25300000768 | tf_op jit(solution)/shard_map/pallas_call | solution.py:887
  261.8 4.4 %collective-permute-done.57.refs_1_ = bf16[2112,128]{1,0:T(8,128)(2,1)S(1)} collective-permute-done((bf16[2112,128]{1,0:T(8,128)(2,1)S(1)}, bf16[2112,128]{1,0:T(8,128)(2,1)S(1)}, u32[]{:S(2)}, u32[]{:S(2)}) %collective-permute-start.57) | collective-permute-done | bytes 540704 | tf_op jit(solution)/shard_map/ppermute | solution.py:38
  266.2 3.1 collective-permute-start.46
  269.5 11.6 %collective-permute-done.58.refs_2_ = bf16[2112,128]{1,0:T(8,128)(2,1)S(1)} collective-permute-done((bf16[2112,128]{1,0:T(8,128)(2,1)S(1)}, bf16[2112,128]{1,0:T(8,128)(2,1)S(1)}, u32[]{:S(2)}, u32[]{:S(2)}) %collective-permute-start.58) | collective-permute-done | bytes 540704 | tf_op jit(solution)/shard_map/ppermute | solution.py:38
  288.4 4.0 %collective-permute-done.40.m2 = bf16[512,512]{1,0:T(8,128)(2,1)S(1)} collective-permute-done((bf16[512,512]{1,0:T(8,128)(2,1)S(1)}, bf16[512,512]{1,0:T(8,128)(2,1)S(1)}, u32[]{:S(2)}, u32[]{:S(2)}) %collective-permute-start.40) | collective-permute-done | bytes 524320 | tf_op jit(solution)/shard_map/ppermute | solution.py:46
  305.0 6.5 %collective-permute-start.63 = (f32[1,128]{1,0:T(1,128)S(1)}, f32[1,128]{1,0:T(1,128)S(1)}, u32[]{:S(2)}, u32[]{:S(2)}) collective-permute-start(f32[1,128]{1,0:T(1,128)S(1)} %maximum_bitcast_fusion), channel_id=1, source_target_pairs={{0,3},{1,2},{2,1},{3,0},{4,7},{5,6},{6,5},{7,4},{8,11},{9,10},{10,... | collective-permute-start | bytes 1544 | tf_op jit(solution)/shard_map/ppermute | solution.py:58
  (304 shorter events, 135.6 us)
Async XLA Ops:
  29.6 17.0 %collective-permute-start.8 = (bf16[4,1184,128]{2,1,0:T(8,128)(2,1)S(1)}, bf16[4,1184,128]{2,1,0:T(8,128)(2,1)}, u32[]{:S(2)}, u32[]{:S(2)}) collective-permute-start(bf16[4,1184,128]{2,1,0:T(8,128)(2,1)S(1)} %shard_map.198.refs_0_.refs_22_), channel_id=1, source_target_pairs={{0,96},{1,13},{4,100},{5,9},{8,104},{9,5},{12,108},{13,1},{32,64},... | collective-permute-start | bytes 3637256 | tf_op jit(solution)/shard_map/ppermute | solution.py:38
  31.8 19.2 %collective-permute-start.1 = (bf16[512,512]{1,0:T(8,128)(2,1)S(1)}, bf16[512,512]{1,0:T(8,128)(2,1)}, u32[]{:S(2)}, u32[]{:S(2)}) collective-permute-start(bf16[512,512]{1,0:T(8,128)(2,1)S(1)} %get-tuple-element.95.x0.refs_27_.x), channel_id=1, source_target_pairs={{0,2},{2,0},{1,3},{3,1},{4,6},{6,4},{5,7},{7,5},{8,10},{10,8},{9,1... | collective-permute-start | bytes 1572872 | tf_op jit(solution)/shard_map/ppermute | solution.py:54
  34.6 28.3 %collective-permute-start = (bf16[512,512]{1,0:T(8,128)(2,1)S(1)}, bf16[512,512]{1,0:T(8,128)(2,1)}, u32[]{:S(2)}, u32[]{:S(2)}) collective-permute-start(bf16[512,512]{1,0:T(8,128)(2,1)S(1)} %get-tuple-element.95.x0.refs_27_.x), channel_id=1, source_target_pairs={{0,1},{1,0},{2,3},{3,2},{4,5},{5,4},{6,7},{7,6},{8,9},{9,8},{10,11... | collective-permute-start | bytes 1572872 | tf_op jit(solution)/shard_map/ppermute | solution.py:50
  40.6 17.5 %collective-permute-start.25 = (bf16[1056,128]{1,0:T(8,128)(2,1)}, bf16[1056,128]{1,0:T(8,128)(2,1)}, u32[]{:S(2)}, u32[]{:S(2)}) collective-permute-start(bf16[1056,128]{1,0:T(8,128)(2,1)} %get-tuple-element.97.refs_0_.refs_4_), channel_id=1, source_target_pairs={{0,16},{16,0},{1,17},{17,1},{2,18},{18,2},{3,19},{19,3},{4,20},{20... | collective-permute-start | bytes 811016 | tf_op jit(solution)/shard_map/ppermute | solution.py:62
  51.0 16.5 %collective-permute-start.10 = (bf16[2,1184,128]{2,1,0:T(8,128)(2,1)}, bf16[2,1184,128]{2,1,0:T(8,128)(2,1)}, u32[]{:S(2)}, u32[]{:S(2)}) collective-permute-start(bf16[2,1184,128]{2,1,0:T(8,128)(2,1)} %get-tuple-element.99), channel_id=1, source_target_pairs={{0,32},{1,5},{4,36},{5,1},{8,40},{9,13},{12,44},{13,9},{32,0},{33,... | collective-permute-start | bytes 1818632 | tf_op jit(solution)/shard_map/ppermute | solution.py:38
  58.1 27.3 %collective-permute-start.20 = (bf16[512,512]{1,0:T(8,128)(2,1)S(1)}, bf16[512,512]{1,0:T(8,128)(2,1)S(1)}, u32[]{:S(2)}, u32[]{:S(2)}) collective-permute-start(bf16[512,512]{1,0:T(8,128)(2,1)S(1)} %get-tuple-element.104.refs_0_.refs_12_.refs_8_), channel_id=1, source_target_pairs={{0,16},{1,19},{2,18},{3,17},{16,0},{17,3},{18,2},{19,1},{4,20},{5,... | collective-permute-start | bytes 1572872 | tf_op jit(solution)/shard_map/ppermute | solution.py:46
  81.2 33.5 %collective-permute-start.29 = (bf16[4,2112,128]{2,1,0:T(8,128)(2,1)S(1)}, bf16[4,2112,128]{2,1,0:T(8,128)(2,1)S(1)}, u32[]{:S(2)}, u32[]{:S(2)}) collective-permute-start(bf16[4,2112,128]{2,1,0:T(8,128)(2,1)S(1)} %shard_map.204.refs_17_.refs_0_), channel_id=1, source_target_pairs={{0,32},{1,5},{4,36},{5,1},{8,40},{9,13},{12,44},{13,9},{32,0},{33,... | collective-permute-start | bytes 6488072 | tf_op jit(solution)/shard_map/ppermute | solution.py:38
  83.2 35.0 %collective-permute-start.30 = (bf16[4,2112,128]{2,1,0:T(8,128)(2,1)S(1)}, bf16[4,2112,128]{2,1,0:T(8,128)(2,1)S(1)}, u32[]{:S(2)}, u32[]{:S(2)}) collective-permute-start(bf16[4,2112,128]{2,1,0:T(8,128)(2,1)S(1)} %shard_map.204.refs_17_.refs_0_), channel_id=1, source_target_pairs={{0,96},{1,13},{4,100},{5,9},{8,104},{9,5},{12,108},{13,1},{32,64},... | collective-permute-start | bytes 6488072 | tf_op jit(solution)/shard_map/ppermute | solution.py:38
  85.5 19.6 %collective-permute-start.22 = (bf16[2,512,512]{2,1,0:T(8,128)(2,1)S(1)}, bf16[2,512,512]{2,1,0:T(8,128)(2,1)S(1)}, u32[]{:S(2)}, u32[]{:S(2)}) collective-permute-start(bf16[2,512,512]{2,1,0:T(8,128)(2,1)S(1)} %shard_map.202), channel_id=1, source_target_pairs={{0,18},{1,17},{2,16},{3,19},{16,2},{17,1},{18,0},{19,3},{4,22},{5,... | collective-permute-start | bytes 3145736 | tf_op jit(solution)/shard_map/ppermute | solution.py:46
  86.1 26.9 %collective-permute-start.12 = (bf16[512,512]{1,0:T(8,128)(2,1)S(1)}, bf16[512,512]{1,0:T(8,128)(2,1)S(1)}, u32[]{:S(2)}, u32[]{:S(2)}) collective-permute-start(bf16[512,512]{1,0:T(8,128)(2,1)S(1)} %get-tuple-element.103), channel_id=1, source_target_pairs={{0,2},{2,0},{1,3},{3,1},{4,6},{6,4},{5,7},{7,5},{8,10},{10,8},{9,1... | collective-permute-start | bytes 1572872 | tf_op jit(solution)/shard_map/ppermute | solution.py:54
  119.5 20.3 %collective-permute-start.31 = (bf16[2,2112,128]{2,1,0:T(8,128)(2,1)S(1)}, bf16[2,2112,128]{2,1,0:T(8,128)(2,1)S(1)}, u32[]{:S(2)}, u32[]{:S(2)}) collective-permute-start(bf16[2,2112,128]{2,1,0:T(8,128)(2,1)S(1)} %get-tuple-element.108), channel_id=1, source_target_pairs={{0,96},{1,13},{4,100},{5,9},{8,104},{9,5},{12,108},{13,1},{32,64},... | collective-permute-start | bytes 3244040 | tf_op jit(solution)/shard_map/ppermute | solution.py:38
  119.5 20.2 %collective-permute-start.32 = (bf16[2,2112,128]{2,1,0:T(8,128)(2,1)S(1)}, bf16[2,2112,128]{2,1,0:T(8,128)(2,1)S(1)}, u32[]{:S(2)}, u32[]{:S(2)}) collective-permute-start(bf16[2,2112,128]{2,1,0:T(8,128)(2,1)S(1)} %get-tuple-element.109), channel_id=1, source_target_pairs={{0,32},{1,5},{4,36},{5,1},{8,40},{9,13},{12,44},{13,9},{32,0},{33,... | collective-permute-start | bytes 3244040 | tf_op jit(solution)/shard_map/ppermute | solution.py:38
  169.2 20.3 %collective-permute-start.34 = (bf16[512,512]{1,0:T(8,128)(2,1)S(1)}, bf16[512,512]{1,0:T(8,128)(2,1)S(1)}, u32[]{:S(2)}, u32[]{:S(2)}) collective-permute-start(bf16[512,512]{1,0:T(8,128)(2,1)S(1)} %get-tuple-element.114.refs_0_), channel_id=1, source_target_pairs={{0,16},{1,19},{2,18},{3,17},{16,0},{17,3},{18,2},{19,1},{4,20},{5,... | collective-permute-start | bytes 1572872 | tf_op jit(solution)/shard_map/ppermute | solution.py:46
  172.2 17.2 %collective-permute-start.35 = (bf16[512,512]{1,0:T(8,128)(2,1)S(1)}, bf16[512,512]{1,0:T(8,128)(2,1)S(1)}, u32[]{:S(2)}, u32[]{:S(2)}) collective-permute-start(bf16[512,512]{1,0:T(8,128)(2,1)S(1)} %get-tuple-element.115), channel_id=1, source_target_pairs={{0,18},{1,17},{2,16},{3,19},{16,2},{17,1},{18,0},{19,3},{4,22},{5,... | collective-permute-start | bytes 1572872 | tf_op jit(solution)/shard_map/ppermute | solution.py:46
  172.2 24.3 %collective-permute-start.36 = (bf16[512,512]{1,0:T(8,128)(2,1)S(1)}, bf16[512,512]{1,0:T(8,128)(2,1)S(1)}, u32[]{:S(2)}, u32[]{:S(2)}) collective-permute-start(bf16[512,512]{1,0:T(8,128)(2,1)S(1)} %get-tuple-element.116), channel_id=1, source_target_pairs={{0,2},{2,0},{1,3},{3,1},{4,6},{6,4},{5,7},{7,5},{8,10},{10,8},{9,1... | collective-permute-start | bytes 1572872 | tf_op jit(solution)/shard_map/ppermute | solution.py:54
  196.9 18.4 %collective-permute-start.41 = (bf16[512,512]{1,0:T(8,128)(2,1)S(1)}, bf16[512,512]{1,0:T(8,128)(2,1)S(1)}, u32[]{:S(2)}, u32[]{:S(2)}) collective-permute-start(bf16[512,512]{1,0:T(8,128)(2,1)S(1)} %shard_map.208.refs_5_.refs_0_), channel_id=1, source_target_pairs={{0,1},{1,0},{2,3},{3,2},{4,5},{5,4},{6,7},{7,6},{8,9},{9,8},{10,11... | collective-permute-start | bytes 1572872 | tf_op jit(solution)/shard_map/ppermute | solution.py:50
  212.7 29.1 %collective-permute-start.38 = (bf16[4,512,512]{2,1,0:T(8,128)(2,1)S(1)}, bf16[4,512,512]{2,1,0:T(8,128)(2,1)}, u32[]{:S(2)}, u32[]{:S(2)}) collective-permute-start(bf16[4,512,512]{2,1,0:T(8,128)(2,1)S(1)} %get-tuple-element.120), channel_id=1, source_target_pairs={{0,1},{1,0},{2,3},{3,2},{4,5},{5,4},{6,7},{7,6},{8,9},{9,8},{10,11... | collective-permute-start | bytes 6291464 | tf_op jit(solution)/shard_map/ppermute | solution.py:50
  214.6 31.9 %collective-permute-start.49 = (bf16[4,2112,128]{2,1,0:T(8,128)(2,1)S(1)}, bf16[4,2112,128]{2,1,0:T(8,128)(2,1)}, u32[]{:S(2)}, u32[]{:S(2)}) collective-permute-start(bf16[4,2112,128]{2,1,0:T(8,128)(2,1)S(1)} %get-tuple-element.143.refs_32_), channel_id=1, source_target_pairs={{0,32},{1,5},{4,36},{5,1},{8,40},{9,13},{12,44},{13,9},{32,0},{33,... | collective-permute-start | bytes 6488072 | tf_op jit(solution)/shard_map/ppermute | solution.py:38
  214.7 31.8 %collective-permute-start.50 = (bf16[4,2112,128]{2,1,0:T(8,128)(2,1)S(1)}, bf16[4,2112,128]{2,1,0:T(8,128)(2,1)}, u32[]{:S(2)}, u32[]{:S(2)}) collective-permute-start(bf16[4,2112,128]{2,1,0:T(8,128)(2,1)S(1)} %get-tuple-element.155), channel_id=1, source_target_pairs={{0,96},{1,13},{4,100},{5,9},{8,104},{9,5},{12,108},{13,1},{32,64},... | collective-permute-start | bytes 6488072 | tf_op jit(solution)/shard_map/ppermute | solution.py:38
  252.7 31.3 %collective-permute-start.51 = (bf16[4,1152,128]{2,1,0:T(8,128)(2,1)S(1)}, bf16[4,1152,128]{2,1,0:T(8,128)(2,1)S(1)}, u32[]{:S(2)}, u32[]{:S(2)}) collective-permute-start(bf16[4,1152,128]{2,1,0:T(8,128)(2,1)S(1)} %get-tuple-element.157.refs_4_), channel_id=1, source_target_pairs={{0,32},{1,5},{4,36},{5,1},{8,40},{9,13},{12,44},{13,9},{32,0},{33,... | collective-permute-start | bytes 3538952 | tf_op jit(solution)/shard_map/ppermute | solution.py:38
  252.9 31.1 %collective-permute-start.52 = (bf16[4,1152,128]{2,1,0:T(8,128)(2,1)S(1)}, bf16[4,1152,128]{2,1,0:T(8,128)(2,1)S(1)}, u32[]{:S(2)}, u32[]{:S(2)}) collective-permute-start(bf16[4,1152,128]{2,1,0:T(8,128)(2,1)S(1)} %get-tuple-element.158), channel_id=1, source_target_pairs={{0,96},{1,13},{4,100},{5,9},{8,104},{9,5},{12,108},{13,1},{32,64},... | collective-permute-start | bytes 3538952 | tf_op jit(solution)/shard_map/ppermute | solution.py:38
  254.5 26.6 %collective-permute-start.58 = (bf16[2112,128]{1,0:T(8,128)(2,1)S(1)}, bf16[2112,128]{1,0:T(8,128)(2,1)S(1)}, u32[]{:S(2)}, u32[]{:S(2)}) collective-permute-start(bf16[2112,128]{1,0:T(8,128)(2,1)S(1)} %get-tuple-element.171), channel_id=1, source_target_pairs={{0,8},{1,65},{4,12},{5,69},{8,0},{9,73},{12,4},{13,77},{32,40},{33... | collective-permute-start | bytes 1622024 | tf_op jit(solution)/shard_map/ppermute | solution.py:38
  259.6 23.4 %collective-permute-start.59 = (bf16[2112,128]{1,0:T(8,128)(2,1)S(1)}, bf16[2112,128]{1,0:T(8,128)(2,1)S(1)}, u32[]{:S(2)}, u32[]{:S(2)}) collective-permute-start(bf16[2112,128]{1,0:T(8,128)(2,1)S(1)} %get-tuple-element.172), channel_id=1, source_target_pairs={{0,12},{1,97},{4,8},{5,101},{8,4},{9,105},{12,0},{13,109},{32,44},... | collective-permute-start | bytes 1622024 | tf_op jit(solution)/shard_map/ppermute | solution.py:38
  266.2 17.7 %collective-permute-start.46 = (bf16[528,512]{1,0:T(8,128)(2,1)S(1)}, bf16[528,512]{1,0:T(8,128)(2,1)S(1)}, u32[]{:S(2)}, u32[]{:S(2)}) collective-permute-start(bf16[528,512]{1,0:T(8,128)(2,1)S(1)} %get-tuple-element.148), channel_id=1, source_target_pairs={{0,2},{2,0},{1,3},{3,1},{4,6},{6,4},{5,7},{7,5},{8,10},{10,8},{9,1... | collective-permute-start | bytes 1622024 | tf_op jit(solution)/shard_map/ppermute | solution.py:54
  (118 other events, 1227.7 us)

commit v3 on v2

--- a/solution.py
+++ b/solution.py
@@ -666,11 +666,12 @@
         r_o[...] = r
         n[part] = narrow(hidden * r * wide(gains[1:2, :]))
         save(n.at[part], n_o.at[tokens])
-        if part == 0:
-            wait(copies)
+
+    wait(copies)
+    wait(wd_copies)
+    for part in range(2):
+        tokens = pl.ds(part * SEQ, SEQ)
         both = nt(w[...], n[part])
-        if part == 0:
-            wait(wd_copies)
         d_out = nt(wd[...], cot[part])
         gate, up = both[:FFN], both[FFN:]
         g = jax.nn.sigmoid(gate)

time: 323 us -> 322 us (level)
  transfers between devices with their start and end apart: 64 -> 64, of which waited for: 27 -> 26; matrix products, arithmetic and copies ran while one was open for 1% -> 1% of each run, Pallas kernels for 21% -> 21%
where the time goes in v3:
time: 322 us; the launch traced here: 316 us
  starting transfers between devices  103 us (32%)
  Pallas kernels  93.6 us (29%)
  waiting for transfers between devices  92.2 us (29%)
  local copies, waits for them, and re-layouts  23.1 us (7%)
    ppermute x28, waiting for transfers between devices, turn(): return lambda v: lax.ppermute(v, ('y', 'z', 'core'), pairs)  40 us
    ppermute x16, starting transfers between devices, swap_core(): return lax.ppermute(v, 'core', [(0, 1), (1, 0)])  38.3 us
    ppermute x9, waiting for transfers between devices, cross(): return lambda v: lax.ppermute(v, ('xl', 'xh', 'core'), pairs)  30.2 us
    ppermute x28, starting transfers between devices, turn(): return lambda v: lax.ppermute(v, ('y', 'z', 'core'), pairs)  29.6 us
    unnamed x156, local copies, waits for them, and re-layouts  22.8 us
    pallas_call x1, Pallas kernels, mlp(): pl.pallas_call(mlp_kernel, in_specs=[SCALARS] * 2 + whole(*h, *cot, gains...  22.4 us
    pallas_call x1, Pallas kernels, attention_back(): pl.pallas_call(attention_back_kernel, in_specs=[SCALARS] + whole(*a, *h,...  19.1 us
    pallas_call x1, Pallas kernels, grads_mlp(): pl.pallas_call(grads_mlp_kernel, in_specs=[SCALARS] + [ANYWHERE] * (4 + l...  13.8 us
  transfers between devices with their start and end apart: 64, of which 26 were waited for; matrix products, arithmetic and copies ran while one was open for 1% of the time, Pallas kernels for 21%

profile of v3, /device:TPU:1, one launch (start us, length us, event | category | flops | bytes accessed | tf_op | source)
XLA Modules:
  0.0 315.9 jit_solution(8710973460363413972)
XLA Ops:
  19.5 5.9 %collective-permute-done.5.refs_2_ = bf16[1184,128]{1,0:T(8,128)(2,1)S(1)} collective-permute-done((bf16[1184,128]{1,0:T(8,128)(2,1)S(1)}, bf16[1184,128]{1,0:T(8,128)(2,1)S(1)}, u32[]{:S(2)}, u32[]{:S(2)}) %collective-permute-start.5) | collective-permute-done | bytes 303136 | tf_op jit(solution)/shard_map/ppermute | solution.py:38
  34.6 6.0 %collective-permute-start = (bf16[512,512]{1,0:T(8,128)(2,1)S(1)}, bf16[512,512]{1,0:T(8,128)(2,1)}, u32[]{:S(2)}, u32[]{:S(2)}) collective-permute-start(bf16[512,512]{1,0:T(8,128)(2,1)S(1)} %get-tuple-element.95.x0.refs_27_.x), channel_id=1, source_target_pairs={{0,1},{1,0},{2,3},{3,2},{4,5},{5,4},{6,7},{7,6},{8,9},{9,8},{10,11... | collective-permute-start | bytes 1572872 | tf_op jit(solution)/shard_map/ppermute | solution.py:50
  40.9 3.2 collective-permute-done.7.a.refs_1_.refs_0_.refs_23_
  51.0 6.7 %collective-permute-start.2 = (bf16[512,512]{1,0:T(8,128)(2,1)}, bf16[512,512]{1,0:T(8,128)(2,1)}, u32[]{:S(2)}, u32[]{:S(2)}) collective-permute-start(bf16[512,512]{1,0:T(8,128)(2,1)} %collective-permute-done.1.x2.refs_29_), channel_id=1, source_target_pairs={{0,1},{1,0},{2,3},{3,2},{4,5},{5,4},{6,7},{7,6},{8,9},{9,8},{10,11... | collective-permute-start | bytes 1572872 | tf_op jit(solution)/shard_map/ppermute | solution.py:50
  67.7 10.6 %shard_map.200 = (bf16[512,2048]{1,0:T(8,128)(2,1)S(1)}, bf16[8,512,512]{2,1,0:T(8,128)(2,1)S(1)}, f32[512,1]{1,0:T(8,128)S(1)}, bf16[512,512]{1,0:T(8,128)(2,1)...) custom-call(s32[16]{0:T(128)S(1)} %reshape.53.table, ...), custom_call_target="tpu_custom_call" | custom-call | flops 16099999744 | tf_op jit(solution)/shard_map/pallas_call | solution.py:617
  86.2 4.5 %collective-permute-start.12 = (bf16[512,512]{1,0:T(8,128)(2,1)S(1)}, bf16[512,512]{1,0:T(8,128)(2,1)S(1)}, u32[]{:S(2)}, u32[]{:S(2)}) collective-permute-start(bf16[512,512]{1,0:T(8,128)(2,1)S(1)} %get-tuple-element.103), channel_id=1, source_target_pairs={{0,2},{2,0},{1,3},{3,1},{4,6},{6,4},{5,7},{7,5},{8,10},{10,8},{9,1... | collective-permute-start | bytes 1572872 | tf_op jit(solution)/shard_map/ppermute | solution.py:54
  90.7 14.5 %collective-permute-done.22.refs_10_.refs_14_ = bf16[2,512,512]{2,1,0:T(8,128)(2,1)S(1)} collective-permute-done((bf16[2,512,512]{2,1,0:T(8,128)(2,1)S(1)}, bf16[2,512,512]{2,1,0:T(8,128)(2,1)S(1)}, u32[]{:S(2)}, u32[]{:S(2)}) %collective-permute-start.22) | collective-permute-done | bytes 1048608 | tf_op jit(solution)/shard_map/ppermute | solution.py:46
  105.3 7.7 %collective-permute-start.23 = (bf16[2,512,512]{2,1,0:T(8,128)(2,1)S(1)}, bf16[2,512,512]{2,1,0:T(8,128)(2,1)S(1)}, u32[]{:S(2)}, u32[]{:S(2)}) collective-permute-start(bf16[2,512,512]{2,1,0:T(8,128)(2,1)S(1)} %collective-permute-done.22.refs_10_.refs_14_), channel_id=1, source_target_pairs={{0,1},{1,0},{2,3},{3,2},{4,5},{5,4},{6,7},{7,6},{8,9},{9,8},{10,11... | collective-permute-start | bytes 3145736 | tf_op jit(solution)/shard_map/ppermute | solution.py:50
  114.7 3.4 %collective-permute-start.13 = (bf16[512,512]{1,0:T(8,128)(2,1)S(1)}, bf16[512,512]{1,0:T(8,128)(2,1)S(1)}, u32[]{:S(2)}, u32[]{:S(2)}) collective-permute-start(bf16[512,512]{1,0:T(8,128)(2,1)S(1)} %get-tuple-element.180.refs_4_), channel_id=1, source_target_pairs={{0,16},{1,19},{2,18},{3,17},{16,0},{17,3},{18,2},{19,1},{4,20},{5,... | collective-permute-start | bytes 1572872 | tf_op jit(solution)/shard_map/ppermute | solution.py:46
  119.7 3.7 %collective-permute-start.17 = (bf16[512,512]{1,0:T(8,128)(2,1)S(1)}, bf16[512,512]{1,0:T(8,128)(2,1)S(1)}, u32[]{:S(2)}, u32[]{:S(2)}) collective-permute-start(bf16[512,512]{1,0:T(8,128)(2,1)S(1)} %get-tuple-element.180.refs_4_), channel_id=1, source_target_pairs={{0,1},{1,0},{2,3},{3,2},{4,5},{5,4},{6,7},{7,6},{8,9},{9,8},{10,11... | collective-permute-start | bytes 1572872 | tf_op jit(solution)/shard_map/ppermute | solution.py:50
  125.4 3.7 %collective-permute-done.15.refs_2_ = bf16[512,512]{1,0:T(8,128)(2,1)S(1)} collective-permute-done((bf16[512,512]{1,0:T(8,128)(2,1)S(1)}, bf16[512,512]{1,0:T(8,128)(2,1)S(1)}, u32[]{:S(2)}, u32[]{:S(2)}) %collective-permute-start.15) | collective-permute-done | bytes 524320 | tf_op jit(solution)/shard_map/ppermute | solution.py:46
  131.3 3.5 %collective-permute-done.18.refs_6_ = bf16[512,512]{1,0:T(8,128)(2,1)S(1)} collective-permute-done((bf16[512,512]{1,0:T(8,128)(2,1)S(1)}, bf16[512,512]{1,0:T(8,128)(2,1)S(1)}, u32[]{:S(2)}, u32[]{:S(2)}) %collective-permute-start.18) | collective-permute-done | bytes 524320 | tf_op jit(solution)/shard_map/ppermute | solution.py:46
  134.7 3.4 %collective-permute-start.19 = (bf16[512,512]{1,0:T(8,128)(2,1)S(1)}, bf16[512,512]{1,0:T(8,128)(2,1)S(1)}, u32[]{:S(2)}, u32[]{:S(2)}) collective-permute-start(bf16[512,512]{1,0:T(8,128)(2,1)S(1)} %collective-permute-done.18.refs_6_), channel_id=1, source_target_pairs={{0,1},{1,0},{2,3},{3,2},{4,5},{5,4},{6,7},{7,6},{8,9},{9,8},{10,11... | collective-permute-start | bytes 1572872 | tf_op jit(solution)/shard_map/ppermute | solution.py:50
  139.8 22.4 %shard_map.206 = (f32[512,1]{1,0:T(8,128)S(1)}, bf16[1024,2048]{1,0:T(8,128)(2,1)}, bf16[1024,2048]{1,0:T(8,128)(2,1)}, bf16[704,1024]{1,0:T(8,128)(2,1)S(1)}, b...) custom-call(s32[16]{0:T(128)S(1)} %reshape.53.table, s32[7]{0:T(128)S(1)} %stack.31.where, ...), custom_call_target="tpu_custom_call" | custom-call | flops 34500001792 | tf_op jit(solution)/shard_map/pallas_call | solution.py:701
  162.7 4.0 %collective-permute-done.33.b = bf16[4,512,512]{2,1,0:T(8,128)(2,1)S(1)} collective-permute-done((bf16[4,512,512]{2,1,0:T(8,128)(2,1)}, bf16[4,512,512]{2,1,0:T(8,128)(2,1)S(1)}, u32[]{:S(2)}, u32[]{:S(2)}) %collective-permute-start.33) | collective-permute-done | bytes 2097184 | tf_op jit(solution)/shard_map/ppermute | solution.py:50
  175.3 13.8 %shard_map.214 = (bf16[2,2112,128]{2,1,0:T(8,128)(2,1)S(1)}, bf16[2,2112,128]{2,1,0:T(8,128)(2,1)S(1)}, bf16[4,2112,128]{2,1,0:T(8,128)(2,1)S(1)}, bf16[4,2112,1...) custom-call(s32[16]{0:T(128)S(1)} %reshape.53.table, bf16[1408,1024]{1,0:T(8,128)(2,1)S(1)} %copy-done.63, ...), custom_call_target="tpu_custom_call" | custom-call | flops 17250000896 | tf_op jit(solution)/shard_map/pallas_call | solution.py:789
  189.1 7.0 %collective-permute-done.36.d = bf16[512,512]{1,0:T(8,128)(2,1)S(1)} collective-permute-done((bf16[512,512]{1,0:T(8,128)(2,1)S(1)}, bf16[512,512]{1,0:T(8,128)(2,1)S(1)}, u32[]{:S(2)}, u32[]{:S(2)}) %collective-permute-start.36) | collective-permute-done | bytes 524320 | tf_op jit(solution)/shard_map/ppermute | solution.py:54
  201.2 5.1 %shard_map.209 = (bf16[4,512,512]{2,1,0:T(8,128)(2,1)S(1)}, bf16[4,512,512]{2,1,0:T(8,128)(2,1)S(1)}) custom-call(s32[16]{0:T(128)S(1)} %reshape.53.table, s32[7]{0:T(128)S(1)} %stack.31.where, bf16[704,1024]{1,0:T(8,128)(2,1)S(1)} %copy-done.60, bf16[4,2112,128]{2,1,0:T(8,128)(2,1)S(1)} %copy-done.15, bf16[4,2112,128]{2,1,0:T(8,128)(2,1)S(1)} %copy-done.17, ...), custom_call_target="tpu_custom_call" | custom-call | flops 8049999872 | tf_op jit(solution)/shard_map/pallas_call | solution.py:737
  206.3 4.0 %collective-permute-done.37.refs_0_ = bf16[512,512]{1,0:T(8,128)(2,1)S(1)} collective-permute-done((bf16[512,512]{1,0:T(8,128)(2,1)S(1)}, bf16[512,512]{1,0:T(8,128)(2,1)S(1)}, u32[]{:S(2)}, u32[]{:S(2)}) %collective-permute-start.37) | collective-permute-done | bytes 524320 | tf_op jit(solution)/shard_map/ppermute | solution.py:54
  218.4 19.1 %shard_map.217 = (f32[512,512]{1,0:T(8,128)S(1)}, bf16[2,528,512]{2,1,0:T(8,128)(2,1)S(1)}, bf16[2,528,512]{2,1,0:T(8,128)(2,1)S(1)}, bf16[2,1152,128]{2,1,0:T(8...) custom-call(s32[16]{0:T(128)S(1)} %reshape.53.table, ...), custom_call_target="tpu_custom_call" | custom-call | flops 25300000768 | tf_op jit(solution)/shard_map/pallas_call | solution.py:888
  261.4 4.4 %collective-permute-done.57.refs_1_ = bf16[2112,128]{1,0:T(8,128)(2,1)S(1)} collective-permute-done((bf16[2112,128]{1,0:T(8,128)(2,1)S(1)}, bf16[2112,128]{1,0:T(8,128)(2,1)S(1)}, u32[]{:S(2)}, u32[]{:S(2)}) %collective-permute-start.57) | collective-permute-done | bytes 540704 | tf_op jit(solution)/shard_map/ppermute | solution.py:38
  269.1 11.6 %collective-permute-done.58.refs_2_ = bf16[2112,128]{1,0:T(8,128)(2,1)S(1)} collective-permute-done((bf16[2112,128]{1,0:T(8,128)(2,1)S(1)}, bf16[2112,128]{1,0:T(8,128)(2,1)S(1)}, u32[]{:S(2)}, u32[]{:S(2)}) %collective-permute-start.58) | collective-permute-done | bytes 540704 | tf_op jit(solution)/shard_map/ppermute | solution.py:38
  287.9 4.0 %collective-permute-done.40.m2 = bf16[512,512]{1,0:T(8,128)(2,1)S(1)} collective-permute-done((bf16[512,512]{1,0:T(8,128)(2,1)S(1)}, bf16[512,512]{1,0:T(8,128)(2,1)S(1)}, u32[]{:S(2)}, u32[]{:S(2)}) %collective-permute-start.40) | collective-permute-done | bytes 524320 | tf_op jit(solution)/shard_map/ppermute | solution.py:46
  304.6 6.5 %collective-permute-start.63 = (f32[1,128]{1,0:T(1,128)S(1)}, f32[1,128]{1,0:T(1,128)S(1)}, u32[]{:S(2)}, u32[]{:S(2)}) collective-permute-start(f32[1,128]{1,0:T(1,128)S(1)} %maximum_bitcast_fusion), channel_id=1, source_target_pairs={{0,3},{1,2},{2,1},{3,0},{4,7},{5,6},{6,5},{7,4},{8,11},{9,10},{10,... | collective-permute-start | bytes 1544 | tf_op jit(solution)/shard_map/ppermute | solution.py:58
  (304 shorter events, 135.5 us)
Async XLA Ops:
  29.6 17.0 %collective-permute-start.8 = (bf16[4,1184,128]{2,1,0:T(8,128)(2,1)S(1)}, bf16[4,1184,128]{2,1,0:T(8,128)(2,1)}, u32[]{:S(2)}, u32[]{:S(2)}) collective-permute-start(bf16[4,1184,128]{2,1,0:T(8,128)(2,1)S(1)} %shard_map.198.refs_0_.refs_22_), channel_id=1, source_target_pairs={{0,96},{1,13},{4,100},{5,9},{8,104},{9,5},{12,108},{13,1},{32,64},... | collective-permute-start | bytes 3637256 | tf_op jit(solution)/shard_map/ppermute | solution.py:38
  31.8 19.2 %collective-permute-start.1 = (bf16[512,512]{1,0:T(8,128)(2,1)S(1)}, bf16[512,512]{1,0:T(8,128)(2,1)}, u32[]{:S(2)}, u32[]{:S(2)}) collective-permute-start(bf16[512,512]{1,0:T(8,128)(2,1)S(1)} %get-tuple-element.95.x0.refs_27_.x), channel_id=1, source_target_pairs={{0,2},{2,0},{1,3},{3,1},{4,6},{6,4},{5,7},{7,5},{8,10},{10,8},{9,1... | collective-permute-start | bytes 1572872 | tf_op jit(solution)/shard_map/ppermute | solution.py:54
  34.6 28.3 %collective-permute-start = (bf16[512,512]{1,0:T(8,128)(2,1)S(1)}, bf16[512,512]{1,0:T(8,128)(2,1)}, u32[]{:S(2)}, u32[]{:S(2)}) collective-permute-start(bf16[512,512]{1,0:T(8,128)(2,1)S(1)} %get-tuple-element.95.x0.refs_27_.x), channel_id=1, source_target_pairs={{0,1},{1,0},{2,3},{3,2},{4,5},{5,4},{6,7},{7,6},{8,9},{9,8},{10,11... | collective-permute-start | bytes 1572872 | tf_op jit(solution)/shard_map/ppermute | solution.py:50
  40.6 17.5 %collective-permute-start.25 = (bf16[1056,128]{1,0:T(8,128)(2,1)}, bf16[1056,128]{1,0:T(8,128)(2,1)}, u32[]{:S(2)}, u32[]{:S(2)}) collective-permute-start(bf16[1056,128]{1,0:T(8,128)(2,1)} %get-tuple-element.97.refs_0_.refs_4_), channel_id=1, source_target_pairs={{0,16},{16,0},{1,17},{17,1},{2,18},{18,2},{3,19},{19,3},{4,20},{20... | collective-permute-start | bytes 811016 | tf_op jit(solution)/shard_map/ppermute | solution.py:62
  51.0 16.7 %collective-permute-start.10 = (bf16[2,1184,128]{2,1,0:T(8,128)(2,1)}, bf16[2,1184,128]{2,1,0:T(8,128)(2,1)}, u32[]{:S(2)}, u32[]{:S(2)}) collective-permute-start(bf16[2,1184,128]{2,1,0:T(8,128)(2,1)} %get-tuple-element.99), channel_id=1, source_target_pairs={{0,32},{1,5},{4,36},{5,1},{8,40},{9,13},{12,44},{13,9},{32,0},{33,... | collective-permute-start | bytes 1818632 | tf_op jit(solution)/shard_map/ppermute | solution.py:38
  58.1 27.5 %collective-permute-start.20 = (bf16[512,512]{1,0:T(8,128)(2,1)S(1)}, bf16[512,512]{1,0:T(8,128)(2,1)S(1)}, u32[]{:S(2)}, u32[]{:S(2)}) collective-permute-start(bf16[512,512]{1,0:T(8,128)(2,1)S(1)} %get-tuple-element.104.refs_0_.refs_12_.refs_8_), channel_id=1, source_target_pairs={{0,16},{1,19},{2,18},{3,17},{16,0},{17,3},{18,2},{19,1},{4,20},{5,... | collective-permute-start | bytes 1572872 | tf_op jit(solution)/shard_map/ppermute | solution.py:46
  81.4 33.3 %collective-permute-start.29 = (bf16[4,2112,128]{2,1,0:T(8,128)(2,1)S(1)}, bf16[4,2112,128]{2,1,0:T(8,128)(2,1)S(1)}, u32[]{:S(2)}, u32[]{:S(2)}) collective-permute-start(bf16[4,2112,128]{2,1,0:T(8,128)(2,1)S(1)} %shard_map.204.refs_17_.refs_0_), channel_id=1, source_target_pairs={{0,32},{1,5},{4,36},{5,1},{8,40},{9,13},{12,44},{13,9},{32,0},{33,... | collective-permute-start | bytes 6488072 | tf_op jit(solution)/shard_map/ppermute | solution.py:38
  83.2 35.0 %collective-permute-start.30 = (bf16[4,2112,128]{2,1,0:T(8,128)(2,1)S(1)}, bf16[4,2112,128]{2,1,0:T(8,128)(2,1)S(1)}, u32[]{:S(2)}, u32[]{:S(2)}) collective-permute-start(bf16[4,2112,128]{2,1,0:T(8,128)(2,1)S(1)} %shard_map.204.refs_17_.refs_0_), channel_id=1, source_target_pairs={{0,96},{1,13},{4,100},{5,9},{8,104},{9,5},{12,108},{13,1},{32,64},... | collective-permute-start | bytes 6488072 | tf_op jit(solution)/shard_map/ppermute | solution.py:38
  85.6 19.6 %collective-permute-start.22 = (bf16[2,512,512]{2,1,0:T(8,128)(2,1)S(1)}, bf16[2,512,512]{2,1,0:T(8,128)(2,1)S(1)}, u32[]{:S(2)}, u32[]{:S(2)}) collective-permute-start(bf16[2,512,512]{2,1,0:T(8,128)(2,1)S(1)} %shard_map.202), channel_id=1, source_target_pairs={{0,18},{1,17},{2,16},{3,19},{16,2},{17,1},{18,0},{19,3},{4,22},{5,... | collective-permute-start | bytes 3145736 | tf_op jit(solution)/shard_map/ppermute | solution.py:46
  86.2 26.7 %collective-permute-start.12 = (bf16[512,512]{1,0:T(8,128)(2,1)S(1)}, bf16[512,512]{1,0:T(8,128)(2,1)S(1)}, u32[]{:S(2)}, u32[]{:S(2)}) collective-permute-start(bf16[512,512]{1,0:T(8,128)(2,1)S(1)} %get-tuple-element.103), channel_id=1, source_target_pairs={{0,2},{2,0},{1,3},{3,1},{4,6},{6,4},{5,7},{7,5},{8,10},{10,8},{9,1... | collective-permute-start | bytes 1572872 | tf_op jit(solution)/shard_map/ppermute | solution.py:54
  119.5 20.3 %collective-permute-start.31 = (bf16[2,2112,128]{2,1,0:T(8,128)(2,1)S(1)}, bf16[2,2112,128]{2,1,0:T(8,128)(2,1)S(1)}, u32[]{:S(2)}, u32[]{:S(2)}) collective-permute-start(bf16[2,2112,128]{2,1,0:T(8,128)(2,1)S(1)} %get-tuple-element.108), channel_id=1, source_target_pairs={{0,96},{1,13},{4,100},{5,9},{8,104},{9,5},{12,108},{13,1},{32,64},... | collective-permute-start | bytes 3244040 | tf_op jit(solution)/shard_map/ppermute | solution.py:38
  119.5 20.2 %collective-permute-start.32 = (bf16[2,2112,128]{2,1,0:T(8,128)(2,1)S(1)}, bf16[2,2112,128]{2,1,0:T(8,128)(2,1)S(1)}, u32[]{:S(2)}, u32[]{:S(2)}) collective-permute-start(bf16[2,2112,128]{2,1,0:T(8,128)(2,1)S(1)} %get-tuple-element.109), channel_id=1, source_target_pairs={{0,32},{1,5},{4,36},{5,1},{8,40},{9,13},{12,44},{13,9},{32,0},{33,... | collective-permute-start | bytes 3244040 | tf_op jit(solution)/shard_map/ppermute | solution.py:38
  168.8 20.3 %collective-permute-start.34 = (bf16[512,512]{1,0:T(8,128)(2,1)S(1)}, bf16[512,512]{1,0:T(8,128)(2,1)S(1)}, u32[]{:S(2)}, u32[]{:S(2)}) collective-permute-start(bf16[512,512]{1,0:T(8,128)(2,1)S(1)} %get-tuple-element.114.refs_0_), channel_id=1, source_target_pairs={{0,16},{1,19},{2,18},{3,17},{16,0},{17,3},{18,2},{19,1},{4,20},{5,... | collective-permute-start | bytes 1572872 | tf_op jit(solution)/shard_map/ppermute | solution.py:46
  171.8 17.3 %collective-permute-start.35 = (bf16[512,512]{1,0:T(8,128)(2,1)S(1)}, bf16[512,512]{1,0:T(8,128)(2,1)S(1)}, u32[]{:S(2)}, u32[]{:S(2)}) collective-permute-start(bf16[512,512]{1,0:T(8,128)(2,1)S(1)} %get-tuple-element.115), channel_id=1, source_target_pairs={{0,18},{1,17},{2,16},{3,19},{16,2},{17,1},{18,0},{19,3},{4,22},{5,... | collective-permute-start | bytes 1572872 | tf_op jit(solution)/shard_map/ppermute | solution.py:46
  171.8 24.3 %collective-permute-start.36 = (bf16[512,512]{1,0:T(8,128)(2,1)S(1)}, bf16[512,512]{1,0:T(8,128)(2,1)S(1)}, u32[]{:S(2)}, u32[]{:S(2)}) collective-permute-start(bf16[512,512]{1,0:T(8,128)(2,1)S(1)} %get-tuple-element.116), channel_id=1, source_target_pairs={{0,2},{2,0},{1,3},{3,1},{4,6},{6,4},{5,7},{7,5},{8,10},{10,8},{9,1... | collective-permute-start | bytes 1572872 | tf_op jit(solution)/shard_map/ppermute | solution.py:54
  196.4 18.4 %collective-permute-start.41 = (bf16[512,512]{1,0:T(8,128)(2,1)S(1)}, bf16[512,512]{1,0:T(8,128)(2,1)S(1)}, u32[]{:S(2)}, u32[]{:S(2)}) collective-permute-start(bf16[512,512]{1,0:T(8,128)(2,1)S(1)} %shard_map.208.refs_5_.refs_0_), channel_id=1, source_target_pairs={{0,1},{1,0},{2,3},{3,2},{4,5},{5,4},{6,7},{7,6},{8,9},{9,8},{10,11... | collective-permute-start | bytes 1572872 | tf_op jit(solution)/shard_map/ppermute | solution.py:50
  212.3 29.1 %collective-permute-start.38 = (bf16[4,512,512]{2,1,0:T(8,128)(2,1)S(1)}, bf16[4,512,512]{2,1,0:T(8,128)(2,1)}, u32[]{:S(2)}, u32[]{:S(2)}) collective-permute-start(bf16[4,512,512]{2,1,0:T(8,128)(2,1)S(1)} %get-tuple-element.120), channel_id=1, source_target_pairs={{0,1},{1,0},{2,3},{3,2},{4,5},{5,4},{6,7},{7,6},{8,9},{9,8},{10,11... | collective-permute-start | bytes 6291464 | tf_op jit(solution)/shard_map/ppermute | solution.py:50
  214.1 31.9 %collective-permute-start.49 = (bf16[4,2112,128]{2,1,0:T(8,128)(2,1)S(1)}, bf16[4,2112,128]{2,1,0:T(8,128)(2,1)}, u32[]{:S(2)}, u32[]{:S(2)}) collective-permute-start(bf16[4,2112,128]{2,1,0:T(8,128)(2,1)S(1)} %get-tuple-element.143.refs_32_), channel_id=1, source_target_pairs={{0,32},{1,5},{4,36},{5,1},{8,40},{9,13},{12,44},{13,9},{32,0},{33,... | collective-permute-start | bytes 6488072 | tf_op jit(solution)/shard_map/ppermute | solution.py:38
  214.2 31.8 %collective-permute-start.50 = (bf16[4,2112,128]{2,1,0:T(8,128)(2,1)S(1)}, bf16[4,2112,128]{2,1,0:T(8,128)(2,1)}, u32[]{:S(2)}, u32[]{:S(2)}) collective-permute-start(bf16[4,2112,128]{2,1,0:T(8,128)(2,1)S(1)} %get-tuple-element.155), channel_id=1, source_target_pairs={{0,96},{1,13},{4,100},{5,9},{8,104},{9,5},{12,108},{13,1},{32,64},... | collective-permute-start | bytes 6488072 | tf_op jit(solution)/shard_map/ppermute | solution.py:38
  252.2 31.3 %collective-permute-start.51 = (bf16[4,1152,128]{2,1,0:T(8,128)(2,1)S(1)}, bf16[4,1152,128]{2,1,0:T(8,128)(2,1)S(1)}, u32[]{:S(2)}, u32[]{:S(2)}) collective-permute-start(bf16[4,1152,128]{2,1,0:T(8,128)(2,1)S(1)} %get-tuple-element.157.refs_4_), channel_id=1, source_target_pairs={{0,32},{1,5},{4,36},{5,1},{8,40},{9,13},{12,44},{13,9},{32,0},{33,... | collective-permute-start | bytes 3538952 | tf_op jit(solution)/shard_map/ppermute | solution.py:38
  252.5 31.1 %collective-permute-start.52 = (bf16[4,1152,128]{2,1,0:T(8,128)(2,1)S(1)}, bf16[4,1152,128]{2,1,0:T(8,128)(2,1)S(1)}, u32[]{:S(2)}, u32[]{:S(2)}) collective-permute-start(bf16[4,1152,128]{2,1,0:T(8,128)(2,1)S(1)} %get-tuple-element.158), channel_id=1, source_target_pairs={{0,96},{1,13},{4,100},{5,9},{8,104},{9,5},{12,108},{13,1},{32,64},... | collective-permute-start | bytes 3538952 | tf_op jit(solution)/shard_map/ppermute | solution.py:38
  254.1 26.5 %collective-permute-start.58 = (bf16[2112,128]{1,0:T(8,128)(2,1)S(1)}, bf16[2112,128]{1,0:T(8,128)(2,1)S(1)}, u32[]{:S(2)}, u32[]{:S(2)}) collective-permute-start(bf16[2112,128]{1,0:T(8,128)(2,1)S(1)} %get-tuple-element.171), channel_id=1, source_target_pairs={{0,8},{1,65},{4,12},{5,69},{8,0},{9,73},{12,4},{13,77},{32,40},{33... | collective-permute-start | bytes 1622024 | tf_op jit(solution)/shard_map/ppermute | solution.py:38
  259.1 23.4 %collective-permute-start.59 = (bf16[2112,128]{1,0:T(8,128)(2,1)S(1)}, bf16[2112,128]{1,0:T(8,128)(2,1)S(1)}, u32[]{:S(2)}, u32[]{:S(2)}) collective-permute-start(bf16[2112,128]{1,0:T(8,128)(2,1)S(1)} %get-tuple-element.172), channel_id=1, source_target_pairs={{0,12},{1,97},{4,8},{5,101},{8,4},{9,105},{12,0},{13,109},{32,44},... | collective-permute-start | bytes 1622024 | tf_op jit(solution)/shard_map/ppermute | solution.py:38
  265.8 17.7 %collective-permute-start.46 = (bf16[528,512]{1,0:T(8,128)(2,1)S(1)}, bf16[528,512]{1,0:T(8,128)(2,1)S(1)}, u32[]{:S(2)}, u32[]{:S(2)}) collective-permute-start(bf16[528,512]{1,0:T(8,128)(2,1)S(1)} %get-tuple-element.148), channel_id=1, source_target_pairs={{0,2},{2,0},{1,3},{3,1},{4,6},{6,4},{5,7},{7,5},{8,10},{10,8},{9,1... | collective-permute-start | bytes 1622024 | tf_op jit(solution)/shard_map/ppermute | solution.py:54
  (118 other events, 1225.8 us)
